TPU v7x, 128 devices: a whole 4x4x4 slice. The times are simulated.
128 devices in a mesh: seq: 32 (over y, x, z_lo), tile: 4 (over z_hi, core).
Axes of the slice: x: 4, y: 4, z: 4 (z_hi: 2, z_lo: 2; z = z_hi * 2 + z_lo), core: 2. Of those that a mesh axis runs over, the one named last changes fastest.
Arguments:
- query_act: bfloat16 [2, 16, 64, 11520], P(None, None, 'seq', 'tile'), may hold values from -300 to 300
- key_act: bfloat16 [2, 16, 64, 11520], P(None, None, 'seq', 'tile'), may hold values from -10 to 10
- value_act: bfloat16 [2, 16, 64, 11520], P(None, None, 'seq', 'tile'), may hold values from -6 to 6
- residual: bfloat16 [2, 64, 160, 1152], P(None, 'seq', 'tile'), may hold values from -4 to 4
- gate_scale: float32 [1152], replicated, may hold values from 0.5 to 2
- w_out: bfloat16 [1152, 1152], replicated, may hold values from -0.1875 to 0.1875
- w_probe: float32 [1152, 256], replicated, may hold values from -0.1875 to 0.1875
- w_refine: float32 [3, 3, 256], replicated, may hold values from -0.125 to 0.125
- depth_bins: int32 [2, 256, 640], P(None, 'seq', 'tile'), may hold values from 0 to 255
- mom_probe: float32 [1152, 256], P(('seq', 'tile')), may hold values from -320 to 320
- var_probe: float32 [1152, 256], P(('seq', 'tile')), may hold values from 25 to 2500
- mom_refine: float32 [3, 3, 256], replicated, may hold values from -6144 to 6144
- var_refine: float32 [3, 3, 256], replicated, may hold values from 10000 to 1000000
Outputs:
- loss_map: float32 [2, 256, 640], P(None, 'seq', 'tile')
- map_grad: bfloat16 [2, 64, 160, 256], P(None, 'seq', 'tile')
- probe_step: float32 [1152, 256], P(('seq', 'tile'))
- refine_step: float32 [3, 3, 256], replicated
All inputs are finite; a program needn't handle non-finite values.
Results may differ from a plain program's by a relative error of at most 0.019.
Values may be sent and summed in bfloat16 or wider, within the bound.
No kernel may reach another device: no remote copies, remote signals or barrier semaphores. Data moves between devices by JAX's collectives and lax.ppermute only.
A program may use at most 128 MiB of HBM per device.

v0:
```python
import math

import jax
import jax.numpy as jnp
from jax import lax
from jax.sharding import PartitionSpec as P

HD = 72
NBINS = 256
STEP = 10


BETA_ONE = 0.9
BETA_TWO = 0.999
ADAM_EPS = 1e-08
NORM_EPS = 1e-06
FAR_NEGATIVE = -1e30
PRECISE = lax.Precision.HIGHEST


def extended(cells, sides, width):
    for axis, dim in sides:
        count = lax.axis_size(axis)
        ends = count - 1
        head = lax.slice_in_dim(cells, 0, width, axis=dim)
        tail = lax.slice_in_dim(cells, cells.shape[dim] - width, cells.shape[dim], axis=dim)
        cells = jnp.concatenate(
            [
                lax.ppermute(tail, axis, [(i, (i + 1) % count) for i in range(ends)]),
                cells,
                lax.ppermute(head, axis, [((i + 1) % count, i) for i in range(ends)]),
            ],
            axis=dim,
        )
    return cells


def interp_weights(pixel, latent, count_in):
    source = (pixel + 0.5) * 0.25 - 0.5
    offset = source[:, None] - latent[None, :]
    weight = jnp.maximum(0.0, 1.0 - jnp.abs(offset))
    weight = weight + jnp.where(
        latent[None, :] == 0.0, jnp.maximum(0.0, 1.0 - jnp.abs(offset + 1.0)), 0.0
    )
    weight = weight + jnp.where(
        latent[None, :] == count_in - 1.0, jnp.maximum(0.0, 1.0 - jnp.abs(offset - 1.0)), 0.0
    )
    inside = (
        (pixel[:, None] >= 0.0)
        & (pixel[:, None] < 4.0 * count_in)
        & (latent[None, :] >= 0.0)
        & (latent[None, :] < count_in)
    )
    return jnp.where(inside, weight, 0.0)


def refine_taps(upsampled, w_refine, out_rows, out_cols):
    tap_maps = jnp.einsum("fqwp,abp->fabqw", upsampled, w_refine, precision=PRECISE)
    depth = tap_maps[:, 0, 0, :out_rows, :out_cols]
    for tap_row in range(3):
        for tap_col in range(3):
            if tap_row + tap_col > 0:
                depth = (
                    depth
                    + tap_maps[
                        :,
                        tap_row,
                        tap_col,
                        tap_row : tap_row + out_rows,
                        tap_col : tap_col + out_cols,
                    ]
                )
    return depth


def adam_step(grad, moment, second):
    new_moment = BETA_ONE * moment + (1.0 - BETA_ONE) * grad
    new_second = BETA_TWO * second + (1.0 - BETA_TWO) * grad * grad
    return (
        new_moment
        / (1.0 - BETA_ONE**STEP)
        / (jnp.sqrt(new_second / (1.0 - BETA_TWO**STEP)) + ADAM_EPS)
    )


def body(
    query_act,
    key_act,
    value_act,
    residual,
    gate_scale,
    w_out,
    w_probe,
    w_refine,
    depth_bins,
    mom_probe,
    var_probe,
    mom_refine,
    var_refine,
):
    frame_count, head_count, own_rows, flat_width = query_act.shape
    own_cols = flat_width // HD
    seq_count = lax.axis_size("seq")
    tile_count = lax.axis_size("tile")
    per_device = frame_count * head_count // seq_count
    full_rows = own_rows * seq_count
    full_cols = own_cols * tile_count
    score_scale = HD ** (-0.5)
    query_split = query_act.reshape(seq_count, per_device, own_rows, flat_width)
    key_split = key_act.reshape(seq_count, per_device, own_rows, flat_width)
    value_split = value_act.reshape(seq_count, per_device, own_rows, flat_width)
    query_loc = lax.all_to_all(query_split, "seq", split_axis=0, concat_axis=2, tiled=True)
    key_loc = lax.all_to_all(key_split, "seq", split_axis=0, concat_axis=2, tiled=True)
    value_loc = lax.all_to_all(value_split, "seq", split_axis=0, concat_axis=2, tiled=True)
    item_count = query_loc.shape[1]
    query_count = full_rows * own_cols
    queries = query_loc.reshape(item_count, query_count, HD)
    start_top = jnp.full((item_count, query_count), FAR_NEGATIVE, jnp.float32)
    start_total = jnp.zeros((item_count, query_count), jnp.float32)
    start_weighted = jnp.zeros((item_count, query_count, HD), jnp.float32)
    key_part = lax.all_gather(key_loc, "tile", axis=3, tiled=True)
    value_part = lax.all_gather(value_loc, "tile", axis=3, tiled=True)
    span_cols = key_part.shape[3] // HD
    key_count = full_rows * span_cols
    key_rows = key_part.reshape(item_count, key_count, HD)
    value_rows = value_part.reshape(item_count, key_count, HD)
    key_block = math.gcd(key_count, 2048)

    def advance(block_index, inner):
        row_top, row_total, weighted = inner
        key_slab = lax.dynamic_slice_in_dim(key_rows, block_index * key_block, key_block, 1)
        value_slab = lax.dynamic_slice_in_dim(value_rows, block_index * key_block, key_block, 1)
        scores = (
            jnp.einsum("nqd,nkd->nqk", queries, key_slab, preferred_element_type=jnp.float32)
            * score_scale
        )
        new_top = jnp.maximum(row_top, jnp.max(scores, axis=2))
        rescale = jnp.exp(row_top - new_top)
        shifted = jnp.exp(scores - new_top[:, :, None])
        row_total = row_total * rescale + jnp.sum(shifted, axis=2)
        weighted = weighted * rescale[:, :, None] + jnp.einsum(
            "nqk,nkd->nqd",
            shifted.astype(jnp.bfloat16),
            value_slab,
            preferred_element_type=jnp.float32,
        )
        return (new_top, row_total, weighted)

    row_top, row_total, weighted = lax.fori_loop(
        0, key_count // key_block, advance, (start_top, start_total, start_weighted)
    )
    attended = (weighted / row_total[:, :, None]).astype(jnp.bfloat16)
    attended = attended.reshape(1, item_count, full_rows, own_cols * HD)
    merged = lax.all_to_all(attended, "seq", split_axis=2, concat_axis=0, tiled=True)
    merged = merged.reshape(frame_count, head_count, own_rows, own_cols, HD)
    model_width = w_out.shape[0]
    mixed = jnp.einsum(
        "fhrcd,hde->frce",
        merged,
        w_out.reshape(head_count, HD, model_width),
        preferred_element_type=jnp.float32,
    )
    stream = residual.astype(jnp.float32) + gate_scale * mixed
    row_mean = jnp.mean(stream, axis=3, keepdims=True)
    centered = stream - row_mean
    row_var = jnp.mean(centered * centered, axis=3, keepdims=True)
    features = (centered * lax.rsqrt(row_var + NORM_EPS)).astype(jnp.bfloat16)
    probe_bf = w_probe.astype(jnp.bfloat16)
    probe_map = jnp.einsum(
        "frcd,dp->frcp", features, probe_bf, preferred_element_type=jnp.float32
    ).astype(jnp.bfloat16)
    padded_map = extended(probe_map, (("seq", 1), ("tile", 2)), 1)
    seq_pos = lax.axis_index("seq")
    tile_pos = lax.axis_index("tile")
    row_latent = (seq_pos * own_rows - 1 + jnp.arange(own_rows + 2)).astype(jnp.float32)
    row_pixel = (seq_pos * 4 * own_rows - 1 + jnp.arange(4 * own_rows + 2)).astype(jnp.float32)
    col_latent = (tile_pos * own_cols - 1 + jnp.arange(own_cols + 2)).astype(jnp.float32)
    col_pixel = (tile_pos * 4 * own_cols - 1 + jnp.arange(4 * own_cols + 2)).astype(jnp.float32)
    row_weights = interp_weights(row_pixel, row_latent, float(full_rows))
    col_weights = interp_weights(col_pixel, col_latent, float(full_cols))
    up_rows = jnp.einsum(
        "qr,frcp->fqcp", row_weights, padded_map.astype(jnp.float32), precision=PRECISE
    )
    upsampled = jnp.einsum("wc,fqcp->fqwp", col_weights, up_rows, precision=PRECISE)
    pixel_rows = 4 * own_rows
    pixel_cols = 4 * own_cols
    depth = refine_taps(upsampled, w_refine, pixel_rows, pixel_cols)
    target = (depth_bins.astype(jnp.float32) + 0.5) * (4.0 / NBINS) - 2.0
    depth_error = depth - target
    loss_map = depth_error * depth_error
    depth_grad = 2.0 * depth_error
    refine_part = jnp.stack(
        [
            jnp.stack(
                [
                    jnp.einsum(
                        "fyx,fyxp->p",
                        depth_grad,
                        upsampled[
                            :, tap_row : tap_row + pixel_rows, tap_col : tap_col + pixel_cols
                        ],
                        precision=PRECISE,
                    )
                    for tap_col in range(3)
                ]
            )
            for tap_row in range(3)
        ]
    )
    grad_padded = extended(depth_grad, (("seq", 1), ("tile", 2)), 3)
    shifted_grad = jnp.stack(
        [
            jnp.stack(
                [
                    grad_padded[
                        :,
                        2 - tap_row : 2 - tap_row + pixel_rows + 4,
                        2 - tap_col : 2 - tap_col + pixel_cols + 4,
                    ]
                    for tap_col in range(3)
                ],
                axis=1,
            )
            for tap_row in range(3)
        ],
        axis=1,
    )
    up_grad = jnp.einsum("fabqw,abp->fqwp", shifted_grad, w_refine, precision=PRECISE)
    row_wide = (seq_pos * pixel_rows - 2 + jnp.arange(pixel_rows + 4)).astype(jnp.float32)
    row_own = (seq_pos * own_rows + jnp.arange(own_rows)).astype(jnp.float32)
    col_wide = (tile_pos * pixel_cols - 2 + jnp.arange(pixel_cols + 4)).astype(jnp.float32)
    col_own = (tile_pos * own_cols + jnp.arange(own_cols)).astype(jnp.float32)
    row_adjoint = interp_weights(row_wide, row_own, float(full_rows))
    col_adjoint = interp_weights(col_wide, col_own, float(full_cols))
    grad_rows = jnp.einsum("qr,fqwp->frwp", row_adjoint, up_grad, precision=PRECISE)
    map_grad = jnp.einsum("wc,frwp->frcp", col_adjoint, grad_rows, precision=PRECISE).astype(
        jnp.bfloat16
    )
    slab_rows = mom_probe.shape[0]
    probe_part = jnp.einsum("frcd,frcp->dp", features, map_grad, preferred_element_type=jnp.float32)
    probe_total, refine_grad = lax.psum((probe_part, refine_part), ("seq", "tile"))
    probe_grad = lax.dynamic_slice_in_dim(
        probe_total, lax.axis_index(("seq", "tile")) * slab_rows, slab_rows, 0
    )
    probe_step = adam_step(probe_grad, mom_probe, var_probe)
    refine_step = adam_step(refine_grad, mom_refine, var_refine)
    return (loss_map, map_grad, probe_step, refine_step)


def solution(mesh):
    in_specs = (
        P(None, None, "seq", "tile"),
        P(None, None, "seq", "tile"),
        P(None, None, "seq", "tile"),
        P(None, "seq", "tile", None),
        P(),
        P(),
        P(),
        P(),
        P(None, "seq", "tile"),
        P(("seq", "tile"), None),
        P(("seq", "tile"), None),
        P(),
        P(),
    )
    out_specs = (
        P(None, "seq", "tile"),
        P(None, "seq", "tile", None),
        P(("seq", "tile"), None),
        P(),
    )
    return jax.shard_map(body, mesh=mesh, in_specs=in_specs, out_specs=out_specs, check_vma=False)
```

profile of v0, /device:TPU:1, one launch (start us, length us, event | category | flops | bytes accessed | tf_op | source)
XLA Modules:
  0.0 525.9 jit_solution(7689691294684399958)
XLA Ops:
  7.2 18.9 %all_to_all.42 = bf16[32,1,2,2880]{3,2,1,0:T(2,128)(2,1)S(1)} all-to-all(bf16[32,1,2,2880]{3,2,1,0:T(2,128)(2,1)} %bitcast.221), channel_id=1, replica_groups=mesh['seq'=32,'tile'=4] {'seq'}, dimensions={0} | all-to-all | bytes 737280 | tf_op jit(solution)/shard_map/all_to_all | solution.py:113
  29.3 12.8 %all_to_all.43 = bf16[32,1,2,2880]{3,2,1,0:T(2,128)(2,1)S(1)} all-to-all(bf16[32,1,2,2880]{3,2,1,0:T(2,128)(2,1)} %bitcast.222), channel_id=1, replica_groups=mesh['seq'=32,'tile'=4] {'seq'}, dimensions={0} | all-to-all | bytes 737280 | tf_op jit(solution)/shard_map/all_to_all | solution.py:114
  45.3 4.6 all-to-all-start.1
  61.8 21.0 %all-gather.3.cloned.1.call-done = bf16[1,1,64,11520]{2,1,0,3:T(2,128)(2,1)} async-done(((bf16[1,1,64,2880]{2,1,0,3:T(2,128)(2,1)}), bf16[1,1,64,11520]{2,1,0,3:T(2,128)(2,1)}) %all-gather.3.cloned.1.call-update) | async-done | bytes 1474576 | tf_op jit(solution)/shard_map/all_gather | solution.py:121
  82.8 12.0 %copy.20 = bf16[1,1,64,11520]{3,2,1,0:T(8,128)(2,1)} copy(bf16[1,1,64,11520]{2,1,0,3:T(2,128)(2,1)} %all-gather.3.cloned.1.call-done) | data formatting | bytes 2949120 | tf_op jit(solution)/shard_map/all_gather | solution.py:121
  94.9 8.0 %reshape.259 = bf16[1,10240,72]{2,1,0:T(8,128)(2,1)} reshape(bf16[1,1,64,11520]{3,2,1,0:T(8,128)(2,1)} %copy.20) | data formatting | bytes 2949120 | tf_op jit(solution)/shard_map/reshape | solution.py:125
  102.9 28.2 %all-gather.5.cloned.1.call-done = bf16[1,1,64,11520]{2,1,0,3:T(2,128)(2,1)} async-done(((bf16[1,1,64,2880]{2,1,0,3:T(2,128)(2,1)}), bf16[1,1,64,11520]{2,1,0,3:T(2,128)(2,1)}) %all-gather.5.cloned.1.call-update) | async-done | bytes 1474576 | tf_op jit(solution)/shard_map/all_gather | solution.py:122
  131.1 11.9 %copy.22 = bf16[1,1,64,11520]{3,2,1,0:T(8,128)(2,1)} copy(bf16[1,1,64,11520]{2,1,0,3:T(2,128)(2,1)} %all-gather.5.cloned.1.call-done) | data formatting | bytes 2949120 | tf_op jit(solution)/shard_map/all_gather | solution.py:122
  143.0 7.9 %reshape.263 = bf16[1,10240,72]{2,1,0:T(8,128)(2,1)} reshape(bf16[1,1,64,11520]{3,2,1,0:T(8,128)(2,1)} %copy.22) | data formatting | bytes 2949120 | tf_op jit(solution)/shard_map/reshape | solution.py:126
  150.9 102.0 %while.18 = (s32[]{:T(128)}, f32[1,2560]{1,0:T(1,128)S(1)}, f32[1,2560]{1,0:T(1,128)S(1)}, f32[1,2560,72]{1,2,0:T(8,128)S(1)}, bf16[1,10240,72]{2,1,0:T(8,128)(2...) while((s32[]{:T(128)}, f32[1,2560]{1,0:T(1,128)S(1)}, ...), condition=%wide.region_3.0_spmd.clone, body=%wide.region_0.0_spmd.clone.sunk | while | flops 1552460800 | bytes 150153424 | solution.py:149
  162.3 9.1 %fusion.250 = f32[1,2560,72]{1,2,0:T(8,128)S(1)} fusion(f32[2048,2560]{1,0:T(8,128)} %copy-done.1, f32[2560]{0:T(1024)S(1)} %get-tuple-element.262, f32[1,2560,72]{1,2,0:T(8,128)S(1)} %get-tuple-element.278, bf16[1,10240,72]{2,1,0:T(8,128)(2,1)} %get-tuple-element.292, s32[]{:T(128)S(6)} %select_n.124, f32[2560]{0:T(1024)S(1)} %get-tuple-element.263, ...), kind=kOutput, calls=%fused_computation.6.clone.1 | convolution fusion | flops 771256320 | bytes 22990852 | tf_op jit(solution)/shard_map/while/body/eval_jaxpr/nqk,nkd->nqd/dot_general | solution.py:141
  182.7 9.1 %fusion.250 = f32[1,2560,72]{1,2,0:T(8,128)S(1)} fusion(f32[2048,2560]{1,0:T(8,128)} %copy-done.1, f32[2560]{0:T(1024)S(1)} %get-tuple-element.262, f32[1,2560,72]{1,2,0:T(8,128)S(1)} %get-tuple-element.278, bf16[1,10240,72]{2,1,0:T(8,128)(2,1)} %get-tuple-element.292, s32[]{:T(128)S(6)} %select_n.124, f32[2560]{0:T(1024)S(1)} %get-tuple-element.263, ...), kind=kOutput, calls=%fused_computation.6.clone.1 | convolution fusion | flops 771256320 | bytes 22990852 | tf_op jit(solution)/shard_map/while/body/eval_jaxpr/nqk,nkd->nqd/dot_general | solution.py:141
  203.0 9.1 %fusion.250 = f32[1,2560,72]{1,2,0:T(8,128)S(1)} fusion(f32[2048,2560]{1,0:T(8,128)} %copy-done.1, f32[2560]{0:T(1024)S(1)} %get-tuple-element.262, f32[1,2560,72]{1,2,0:T(8,128)S(1)} %get-tuple-element.278, bf16[1,10240,72]{2,1,0:T(8,128)(2,1)} %get-tuple-element.292, s32[]{:T(128)S(6)} %select_n.124, f32[2560]{0:T(1024)S(1)} %get-tuple-element.263, ...), kind=kOutput, calls=%fused_computation.6.clone.1 | convolution fusion | flops 771256320 | bytes 22990852 | tf_op jit(solution)/shard_map/while/body/eval_jaxpr/nqk,nkd->nqd/dot_general | solution.py:141
  223.4 9.1 %fusion.250 = f32[1,2560,72]{1,2,0:T(8,128)S(1)} fusion(f32[2048,2560]{1,0:T(8,128)} %copy-done.1, f32[2560]{0:T(1024)S(1)} %get-tuple-element.262, f32[1,2560,72]{1,2,0:T(8,128)S(1)} %get-tuple-element.278, bf16[1,10240,72]{2,1,0:T(8,128)(2,1)} %get-tuple-element.292, s32[]{:T(128)S(6)} %select_n.124, f32[2560]{0:T(1024)S(1)} %get-tuple-element.263, ...), kind=kOutput, calls=%fused_computation.6.clone.1 | convolution fusion | flops 771256320 | bytes 22990852 | tf_op jit(solution)/shard_map/while/body/eval_jaxpr/nqk,nkd->nqd/dot_general | solution.py:141
  243.7 9.1 %fusion.250 = f32[1,2560,72]{1,2,0:T(8,128)S(1)} fusion(f32[2048,2560]{1,0:T(8,128)} %copy-done.1, f32[2560]{0:T(1024)S(1)} %get-tuple-element.262, f32[1,2560,72]{1,2,0:T(8,128)S(1)} %get-tuple-element.278, bf16[1,10240,72]{2,1,0:T(8,128)(2,1)} %get-tuple-element.292, s32[]{:T(128)S(6)} %select_n.124, f32[2560]{0:T(1024)S(1)} %get-tuple-element.263, ...), kind=kOutput, calls=%fused_computation.6.clone.1 | convolution fusion | flops 771256320 | bytes 22990852 | tf_op jit(solution)/shard_map/while/body/eval_jaxpr/nqk,nkd->nqd/dot_general | solution.py:141
  265.0 7.0 %all-to-all-start.3 = ((bf16[32,2,2880]{2,1,0:T(2,128)(2,1)}), bf16[32,2,2880]{2,1,0:T(2,128)(2,1)}, u32[]{:S(2)}, u32[]{:S(2)}) async-start(bf16[32,2,2880]{2,1,0:T(2,128)(2,1)} %reshape.300), calls=%async_computation.3 | async-start | bytes 753664 | tf_op jit(solution)/shard_map/all_to_all | solution.py:154
  274.4 7.5 %all-to-all-done.3 = bf16[32,2,2880]{2,1,0:T(2,128)(2,1)} async-done(((bf16[32,2,2880]{2,1,0:T(2,128)(2,1)}), bf16[32,2,2880]{2,1,0:T(2,128)(2,1)}, u32[]{:S(2)}, u32[]{:S(2)}) %all-to-all-start.3) | async-done | bytes 368672 | tf_op jit(solution)/shard_map/all_to_all | solution.py:154
  299.9 4.6 collective-permute-start.3
  304.5 12.2 %collective-permute-start.2 = (bf16[2,4,1,256]{3,2,1,0:T(2,128)(2,1)}, bf16[2,4,1,256]{3,2,1,0:T(2,128)(2,1)}, u32[]{:S(2)}, u32[]{:S(2)}) collective-permute-start(bf16[2,4,1,256]{3,2,1,0:T(2,128)(2,1)} %get-tuple-element.174), channel_id=1, source_target_pairs={{0,1},{1,2},{2,3},{4,5},{5,6},{6,7},{8,9},{9,10},{10,11},{12,13},{... | collective-permute-start | bytes 12296 | tf_op jit(solution)/shard_map/ppermute | solution.py:29
  319.6 4.2 fusion.80
  346.7 5.0 collective-permute-start.6
  357.4 5.5 %fusion.46 = f32[2,2,164,256]{3,1,2,0:T(2,128)S(1)} fusion(f32[2,12,164,256]{3,2,1,0:T(8,128)S(1)} %convolution_bitcast_fusion.2, pred[2]{0:T(512)(128)(4,1)S(1)} %copy-done.17, pred[2]{0:T(512)(128)(4,1)S(1)} %copy-done.19, pred[2]{0:T(512)(128)(4,1)S(1)} %copy-done.18, pred[12]{0:T(512)(128)(4,1)S(1)} %copy-done.15, pred[2]{0:T(512)(128)(4,1)S(1)} %copy-done.20, ...), kind=kOutput, calls=%fused_computation.52 | convolution fusion | flops 24183240 | bytes 4702284 | tf_op jit(solution)/shard_map/qr,fqwp->frwp/dot_general | solution.py:235
  367.3 70.1 %psum.15 = f32[3,3,256]{2,1,0:T(4,128)S(1)} all-reduce(f32[3,3,256]{2,1,0:T(4,128)S(1)} %pad_maximum_fusion.4), channel_id=1, replica_groups=mesh['seq'=32,'tile'=4] {'seq','tile'}, use_global_device_ids=true, to_apply=%region_7.8 | all-reduce | flops 2304 | bytes 18432 | tf_op jit(solution)/shard_map/psum | solution.py:241
  438.0 79.6 %all-reduce.2.cloned.1.call-done = f32[1152,256]{1,0:T(8,128)} async-done(((f32[1152,256]{1,0:T(8,128)}), f32[1152,256]{1,0:T(8,128)}) %all-reduce.2.cloned.1.call-update) | async-done | bytes 1179664 | tf_op jit(solution)/shard_map/psum | solution.py:241
  (188 shorter events, 143.9 us)
Async XLA Ops:
  7.2 282.9 %copy-start = (bf16[1152,1152]{1,0:T(8,128)(2,1)S(1)}, bf16[1152,1152]{1,0:T(8,128)(2,1)}, u32[]{:S(2)}) copy-start(bf16[1152,1152]{1,0:T(8,128)(2,1)} %param.20) | copy-start | bytes 7962628
  7.2 75.6 %all-gather.3.cloned.1.call-start = ((), (), s32[]{:S(2)}) async-start(), calls=%async_computation.4 | async-start | bytes 7372800 | tf_op jit(solution)/shard_map/all_gather | solution.py:121
  29.3 101.8 %all-gather.5.cloned.1.call-start = ((), (), s32[]{:S(2)}) async-start(), calls=%async_computation.5 | async-start | bytes 7372800 | tf_op jit(solution)/shard_map/all_gather | solution.py:122
  45.3 13.6 %all-to-all-start.1 = ((bf16[32,1,2,2880]{3,2,1,0:T(2,128)(2,1)}), bf16[32,1,2,2880]{3,2,1,0:T(2,128)(2,1)}, u32[]{:S(2)}, u32[]{:S(2)}) async-start(bf16[32,1,2,2880]{3,2,1,0:T(2,128)(2,1)} %bitcast.223), calls=%async_computation.1 | async-start | bytes 753664 | tf_op jit(solution)/shard_map/all_to_all | solution.py:112
  175.6 7.0 %copy-start.1 = (f32[2048,2560]{1,0:T(8,128)}, f32[2048,2560]{1,0:T(8,128)S(1)}, u32[]{:S(2)}) copy-start(f32[2048,2560]{1,0:T(8,128)S(1)} %get-tuple-element.261) | copy-start | bytes 62914564 | tf_op jit(solution)/shard_map/while
  255.8 34.3 %copy-start.28 = (f32[1152]{0:T(1024)S(1)}, f32[1152]{0:T(1024)}, u32[]{:S(2)}) copy-start(f32[1152]{0:T(1024)} %param.19) | copy-start | bytes 13828
  265.0 16.9 %all-to-all-start.3 = ((bf16[32,2,2880]{2,1,0:T(2,128)(2,1)}), bf16[32,2,2880]{2,1,0:T(2,128)(2,1)}, u32[]{:S(2)}, u32[]{:S(2)}) async-start(bf16[32,2,2880]{2,1,0:T(2,128)(2,1)} %reshape.300), calls=%async_computation.3 | async-start | bytes 753664 | tf_op jit(solution)/shard_map/all_to_all | solution.py:154
  272.1 245.5 %all-reduce.2.cloned.1.call-start = ((), (), s32[]{:S(2)}) async-start(), calls=%async_computation.6 | async-start | bytes 2359296 | tf_op jit(solution)/shard_map/psum | solution.py:241
  292.2 7.1 %copy-start.5 = (f32[2,2,40]{2,1,0:T(2,128)}, f32[2,2,40]{2,1,0:T(2,128)S(1)}, u32[]{:S(2)}) copy-start(f32[2,2,40]{2,1,0:T(2,128)S(1)} %broadcast_multiply_fusion.1) | copy-start | bytes 1924
  292.4 7.5 %copy-start.12 = (f32[2,2,40]{2,1,0:T(2,128)}, f32[2,2,40]{2,1,0:T(2,128)S(1)}, u32[]{:S(2)}) copy-start(f32[2,2,40]{2,1,0:T(2,128)S(1)} %add_rsqrt_fusion) | copy-start | bytes 1924
  292.8 5.8 %collective-permute-start.1 = (bf16[2,1,40,256]{3,2,1,0:T(8,128)(2,1)S(1)}, bf16[2,1,40,256]{3,2,1,0:T(8,128)(2,1)S(1)}, u32[]{:S(2)}, u32[]{:S(2)}) collective-permute-start(bf16[2,1,40,256]{3,2,1,0:T(8,128)(2,1)S(1)} %get-tuple-element.177), channel_id=1, source_target_pairs={{4,0},{8,4},{12,8},{16,12},{20,16},{24,20},{28,24},{32,28},{36,32}... | collective-permute-start | bytes 122888 | tf_op jit(solution)/shard_map/ppermute | solution.py:31
  294.1 5.2 collective-permute-start
  299.9 17.4 %collective-permute-start.3 = (bf16[2,4,1,256]{3,2,1,0:T(2,128)(2,1)}, bf16[2,4,1,256]{3,2,1,0:T(2,128)(2,1)}, u32[]{:S(2)}, u32[]{:S(2)}) collective-permute-start(bf16[2,4,1,256]{3,2,1,0:T(2,128)(2,1)} %get-tuple-element.175), channel_id=1, source_target_pairs={{1,0},{2,1},{3,2},{5,4},{6,5},{7,6},{9,8},{10,9},{11,10},{13,12},{... | collective-permute-start | bytes 12296 | tf_op jit(solution)/shard_map/ppermute | solution.py:31
  304.5 12.7 %collective-permute-start.2 = (bf16[2,4,1,256]{3,2,1,0:T(2,128)(2,1)}, bf16[2,4,1,256]{3,2,1,0:T(2,128)(2,1)}, u32[]{:S(2)}, u32[]{:S(2)}) collective-permute-start(bf16[2,4,1,256]{3,2,1,0:T(2,128)(2,1)} %get-tuple-element.174), channel_id=1, source_target_pairs={{0,1},{1,2},{2,3},{4,5},{5,6},{6,7},{8,9},{9,10},{10,11},{12,13},{... | collective-permute-start | bytes 12296 | tf_op jit(solution)/shard_map/ppermute | solution.py:29
  319.6 7.5 %copy-start.7 = (s32[2,8,160]{2,1,0:T(8,128)S(1)}, s32[2,8,160]{2,1,0:T(8,128)}, u32[]{:S(2)}) copy-start(s32[2,8,160]{2,1,0:T(8,128)} %param.23) | copy-start | bytes 30724
  337.4 7.0 %collective-permute-start.5 = (f32[2,3,160]{2,1,0:T(4,128)S(1)}, f32[2,3,160]{2,1,0:T(4,128)S(1)}, u32[]{:S(2)}, u32[]{:S(2)}) collective-permute-start(f32[2,3,160]{2,1,0:T(4,128)S(1)} %get-tuple-element.192), channel_id=1, source_target_pairs={{4,0},{8,4},{12,8},{16,12},{20,16},{24,20},{28,24},{32,28},{36,32}... | collective-permute-start | bytes 11528 | tf_op jit(solution)/shard_map/ppermute | solution.py:31
  338.7 5.8 %collective-permute-start.4 = (f32[2,3,160]{2,1,0:T(4,128)S(1)}, f32[2,3,160]{2,1,0:T(4,128)S(1)}, u32[]{:S(2)}, u32[]{:S(2)}) collective-permute-start(f32[2,3,160]{2,1,0:T(4,128)S(1)} %get-tuple-element.191), channel_id=1, source_target_pairs={{0,4},{4,8},{8,12},{12,16},{16,20},{20,24},{24,28},{28,32},{32,36}... | collective-permute-start | bytes 11528 | tf_op jit(solution)/shard_map/ppermute | solution.py:29
  344.6 8.8 %collective-permute-start.7 = (f32[2,14,3]{2,1,0:T(8,128)S(1)}, f32[2,14,3]{2,1,0:T(8,128)S(1)}, u32[]{:S(2)}, u32[]{:S(2)}) collective-permute-start(f32[2,14,3]{2,1,0:T(8,128)S(1)} %get-tuple-element.188), channel_id=1, source_target_pairs={{1,0},{2,1},{3,2},{5,4},{6,5},{7,6},{9,8},{10,9},{11,10},{13,12},{... | collective-permute-start | bytes 1016 | tf_op jit(solution)/shard_map/ppermute | solution.py:31
  346.7 6.7 %collective-permute-start.6 = (f32[2,14,3]{2,1,0:T(8,128)S(1)}, f32[2,14,3]{2,1,0:T(8,128)S(1)}, u32[]{:S(2)}, u32[]{:S(2)}) collective-permute-start(f32[2,14,3]{2,1,0:T(8,128)S(1)} %get-tuple-element.187), channel_id=1, source_target_pairs={{0,1},{1,2},{2,3},{4,5},{5,6},{6,7},{8,9},{9,10},{10,11},{12,13},{... | collective-permute-start | bytes 1016 | tf_op jit(solution)/shard_map/ppermute | solution.py:29
  362.9 74.4 %copy-start.10 = (f32[3,3,256]{2,1,0:T(4,128)S(1)}, f32[3,3,256]{2,1,0:T(4,128)}, u32[]{:S(2)}) copy-start(f32[3,3,256]{2,1,0:T(4,128)} %param.27) | copy-start | bytes 27652
  363.0 74.4 %copy-start.11 = (f32[3,3,256]{2,1,0:T(4,128)S(1)}, f32[3,3,256]{2,1,0:T(4,128)}, u32[]{:S(2)}) copy-start(f32[3,3,256]{2,1,0:T(4,128)} %param.26) | copy-start | bytes 27652
  363.0 154.6 %copy-start.8 = (f32[9,256]{1,0:T(8,128)S(1)}, f32[9,256]{1,0:T(8,128)}, u32[]{:S(2)}) copy-start(f32[9,256]{1,0:T(8,128)} %param.25) | copy-start | bytes 27652
  363.0 154.6 %copy-start.9 = (f32[9,256]{1,0:T(8,128)S(1)}, f32[9,256]{1,0:T(8,128)}, u32[]{:S(2)}) copy-start(f32[9,256]{1,0:T(8,128)} %param.24) | copy-start | bytes 27652
  363.7 155.2 %copy-start.3 = (bf16[2,2,40,256]{3,2,1,0:T(8,128)(2,1)}, bf16[2,2,40,256]{3,2,1,0:T(8,128)(2,1)S(1)}, u32[]{:S(2)}) copy-start(bf16[2,2,40,256]{3,2,1,0:T(8,128)(2,1)S(1)} %fusion.52) | copy-start | bytes 245764
  (22 other events, 116.7 us)
Sparse Core Ops, SparseCore 0:
  29.4 53.3 all-gather.2
  84.5 46.5 all-gather.4
  365.4 152.1 all-reduce.1
where the time goes:
time: 535 us; the launch traced here: 526 us
  waiting for transfers between devices  138 us (26%)
  blocking collectives  102 us (19%)
  matrix products  102 us (19%)
  local copies, waits for them, and re-layouts  80.7 us (15%)
  starting transfers between devices  46.2 us (9%)
  other arithmetic  41.8 us (8%)
  between operations  14.8 us (3%)
    psum x1, waiting for transfers between devices, body(): lax.psum((probe_part, refine_part), ('seq', 'tile'))  79.6 us
    psum x1, blocking collectives, body(): lax.psum((probe_part, refine_part), ('seq', 'tile'))  70.1 us
    dot_general x5, matrix products, advance(): jnp.einsum('nqk,nkd->nqd', shifted.astype(jnp.bfloat16), value_slab, pref...  45.6 us
    all_gather x1, waiting for transfers between devices, body(): value_part = lax.all_gather(value_loc, 'tile', axis=3, tiled=True)  28.2 us
    ppermute x4, starting transfers between devices, extended(): lax.ppermute(tail, axis, [(i, (i + 1) % count) for i in range(ends)])  25.1 us
    all_gather x1, waiting for transfers between devices, body(): key_part = lax.all_gather(key_loc, 'tile', axis=3, tiled=True)  21 us
    dot_general x5, matrix products, advance(): jnp.einsum('nqd,nkd->nqk', queries, key_slab, preferred_element_type=jnp....  20.7 us
    reduce_sum x5, other arithmetic, advance(): row_total = row_total * rescale + jnp.sum(shifted, axis=2)  18.9 us
  transfers between devices with their start and end apart: 13, of which 6 were waited for; matrix products, arithmetic and copies ran while one was open for 8% of the time, Pallas kernels for 0%

commit v1 on v0

v1 whole, which is shorter than its diff:
```python
import functools
import math

import jax
import jax.numpy as jnp
from jax import lax
from jax.experimental import pallas as pl
from jax.experimental.pallas import tpu as pltpu
from jax.sharding import Mesh, PartitionSpec as P

HD = 72
HEADS = 16
D = 1152
P_SIZE = 256
NBINS = 256
STEP = 10
ROWS = 64
COLS = 40
TOKENS = ROWS * COLS
BLOCK = 256
SEQ_COUNT = 32
TILE_COUNT = 4
FULL_ROWS = 256
FULL_COLS = 640

BETA_ONE = 0.9
BETA_TWO = 0.999
ADAM_EPS = 1e-08
NORM_EPS = 1e-06
PRECISE = lax.Precision.HIGHEST
EXP_SCALE = HD ** (-0.5) * math.log2(math.e)

SEQ = ("y", "x", "z_lo")
TILE = ("z_hi", "core")
PLANE = ("y", "x")
COLUMN = ("z_lo", "z_hi", "core")

NT = (((1,), (1,)), ((), ()))
TN = (((0,), (0,)), ((), ()))
F32 = jnp.float32
BF16 = jnp.bfloat16
VMEM = pl.BlockSpec(memory_space=pltpu.VMEM)
SMEM = pl.BlockSpec(memory_space=pltpu.SMEM)


def call(kernel, out_shape, operands, scratch=(), flops=0, bytes_accessed=0, transcendentals=0, limit=56):
    in_specs = [SMEM if x.dtype == jnp.int32 and x.ndim == 1 else VMEM for x in operands]
    many = isinstance(out_shape, (list, tuple))
    return pl.pallas_call(
        kernel,
        out_shape=out_shape,
        in_specs=in_specs,
        out_specs=[VMEM] * len(out_shape) if many else VMEM,
        scratch_shapes=list(scratch),
        compiler_params=pltpu.CompilerParams(vmem_limit_bytes=limit * 2**20),
        cost_estimate=pl.CostEstimate(
            flops=flops, bytes_accessed=bytes_accessed, transcendentals=transcendentals
        ),
    )(*operands)


def halves(value):
    high = value.astype(BF16)
    low = (value - high.astype(F32)).astype(BF16)
    return high, low


def unpack(packed, rows):
    for c in range(COLS):
        rows[c * ROWS : (c + 1) * ROWS, :HD] = packed[:, c * HD : (c + 1) * HD]


def attend_kernel(first, last, *refs):
    if first:
        q_ref, kv_ref, query_rows, acc_out, key_rows, value_rows, scores_ref = refs
        query_rows[...] = jnp.zeros_like(query_rows)
        unpack(q_ref, query_rows)
    elif last:
        query_rows, kv_ref, acc_ref, out_ref, key_rows, value_rows, scores_ref, acc_out = refs
    else:
        query_rows, kv_ref, acc_ref, acc_out, key_rows, value_rows, scores_ref = refs
    key_rows[...] = jnp.zeros_like(key_rows)
    lane = lax.broadcasted_iota(jnp.int32, (TOKENS, 128), 1)
    value_rows[...] = jnp.where(lane == HD, 1.0, 0.0).astype(BF16)
    unpack(kv_ref.at[0], key_rows)
    unpack(kv_ref.at[1], value_rows)
    blocks = TOKENS // BLOCK
    block_lane = lax.broadcasted_iota(jnp.int32, (BLOCK, 128), 1)

    def scores(i):
        rows = pl.ds(pl.multiple_of(i * BLOCK, BLOCK), BLOCK)
        return lax.dot_general(query_rows[rows, :], key_rows[...], NT, preferred_element_type=F32)

    def step(i, now, later):
        scores_ref[later] = scores(jnp.minimum(i + 1, blocks - 1))
        rows = pl.ds(pl.multiple_of(i * BLOCK, BLOCK), BLOCK)
        block = scores_ref[now]
        top = jnp.max(block, axis=1, keepdims=True)
        if not first:
            old = acc_ref[rows, :]
            old_top = old[:, HD + 1 : HD + 2]
            top = jnp.maximum(top, old_top)
        weights = jnp.exp2((block - top) * EXP_SCALE).astype(BF16)
        total = jnp.dot(weights, value_rows[...], preferred_element_type=F32)
        if not first:
            total = total + old * jnp.exp2((old_top - top) * EXP_SCALE)
        if last:
            acc_out[rows, :] = total / total[:, HD : HD + 1]
        else:
            acc_out[rows, :] = jnp.where(block_lane == HD + 1, top, total)

    scores_ref[0] = scores(0)

    def pair(j, carry):
        step(2 * j, 0, 1)
        step(2 * j + 1, 1, 0)
        return carry

    lax.fori_loop(0, blocks // 2, pair, 0)
    if last:
        for c in range(COLS):
            out_ref[:, c * HD : (c + 1) * HD] = acc_out[c * ROWS : (c + 1) * ROWS, :HD].astype(BF16)


def attend(first, last, *operands):
    rows = jax.ShapeDtypeStruct((TOKENS, 128), BF16)
    acc = jax.ShapeDtypeStruct((TOKENS, 128), F32)
    if first:
        out = [rows, acc]
    elif last:
        out = jax.ShapeDtypeStruct((ROWS, COLS * HD), BF16)
    else:
        out = acc
    scratch = [
        pltpu.VMEM((TOKENS, 128), BF16),
        pltpu.VMEM((TOKENS, 128), BF16),
        pltpu.VMEM((2, BLOCK, TOKENS), F32),
    ]
    if last:
        scratch.append(pltpu.VMEM((TOKENS, 128), F32))
    return call(
        functools.partial(attend_kernel, first, last),
        out,
        operands,
        scratch,
        flops=4 * TOKENS * TOKENS * 256,
        bytes_accessed=4 * 2**20,
        transcendentals=TOKENS * TOKENS,
    )


def weights_kernel(w_probe, taps, probe_out, tap_weights):
    probe = w_probe[...].astype(BF16)
    probe_out[...] = probe
    high, low = halves(taps[...])
    rest = (taps[...] - high.astype(F32) - low.astype(F32)).astype(BF16)
    folded = lax.dot_general(
        jnp.concatenate([high, low, rest], 0).astype(BF16), probe, NT, preferred_element_type=F32
    )
    folded = folded[:24] + folded[24:48] + folded[48:72]
    tap_high, tap_low = halves(folded)
    tap_weights[...] = jnp.concatenate([tap_high.astype(F32), tap_low.astype(F32)], 0).astype(BF16)


def features_kernel(
    merged, residual, gate, w_out, tap_weights, bins, features_out, tap_maps, spread, joined
):
    for c in range(COLS):
        spread[c * ROWS : (c + 1) * ROWS, :HD] = merged[:, c * HD : (c + 1) * HD].astype(F32)
    for h in range(HEADS):
        for g in range(4):
            f, r = divmod(g, 2)
            piece = spread[pl.ds(f * 2 * HEADS + h * 2 + r, COLS, stride=ROWS), :]
            joined[g * COLS : (g + 1) * COLS, h * HD : (h + 1) * HD] = piece[:, :HD]
    mixed = jnp.dot(joined[...].astype(BF16), w_out[...], preferred_element_type=F32)
    stream = residual[...].astype(F32) + gate[...] * mixed
    centered = stream - jnp.mean(stream, axis=1, keepdims=True)
    var = jnp.mean(centered * centered, axis=1, keepdims=True)
    features = (centered * lax.rsqrt(var + NORM_EPS)).astype(BF16)
    features_out[...] = features
    maps = lax.dot_general(tap_weights[...], features, NT, preferred_element_type=F32)
    maps = maps[:24] + maps[24:48]
    tap_maps[...] = jnp.zeros_like(tap_maps)
    for g in range(4):
        for b in range(3):
            tap_maps[g * 8 : (g + 1) * 8, b * 128 : b * 128 + COLS] = maps[
                b * 8 : (b + 1) * 8, g * COLS : (g + 1) * COLS
            ]
    tap_maps[32:48, :160] = bins[...].astype(F32)


def hat(offset):
    return jnp.maximum(0.0, 1.0 - jnp.abs(offset))


def interp(pixel, latent, count_in):
    source = (pixel.astype(F32) + 0.5) * 0.25 - 0.5
    offset = source - latent.astype(F32)
    weight = hat(offset)
    weight = weight + jnp.where(latent == 0, hat(offset + 1.0), 0.0)
    weight = weight + jnp.where(latent == count_in - 1, hat(offset - 1.0), 0.0)
    inside = (pixel >= 0) & (pixel < 4 * count_in) & (latent >= 0) & (latent < count_in)
    return jnp.where(inside, weight, 0.0)


def col_weights(tile, source):
    shape = (384, 256)
    i = lax.broadcasted_iota(jnp.int32, shape, 0)
    x = lax.broadcasted_iota(jnp.int32, shape, 1)
    tap = i >> 7
    c = i & 127
    weight = interp(tile * 160 - 4 + x + tap, source * COLS + c, TILE_COUNT * COLS)
    return jnp.where(c < COLS, weight, 0.0)


def row_weights(seq, source):
    shape = (32, 32)
    i = lax.broadcasted_iota(jnp.int32, shape, 0)
    j = lax.broadcasted_iota(jnp.int32, shape, 1)
    y = i & 15
    tap = j & 7
    weight = interp(seq * 8 - 4 + y + tap, source * 2 + ((j >> 3) & 1), ROWS)
    return jnp.where(((i >> 4) == (j >> 4)) & (tap < 3), weight, 0.0)


def dot(left, right, dims=None):
    if dims is None:
        dims = (((1,), (0,)), ((), ()))
    return lax.dot_general(left, right, dims, precision=PRECISE, preferred_element_type=F32)


def pick(shape, wanted, there):
    i = lax.broadcasted_iota(jnp.int32, shape, 0)
    j = lax.broadcasted_iota(jnp.int32, shape, 1)
    return jnp.where(wanted(i) == there(j), 1.0, 0.0).astype(BF16)


def widen_kernel(place, own, near, far, out):
    tile = place[1]
    maps = jnp.zeros((32, 256), F32)
    bins = jnp.zeros((16, 256), F32)
    for block, source in ((own, tile), (near, place[3]), (far, place[5])):
        maps = maps + dot(block[:32, :], col_weights(tile, source))
        move = pick((160, 256), lambda i: source * 160 + i, lambda j: tile * 160 - 3 + j)
        bins = bins + jnp.dot(
            block[32:48, :160].astype(BF16), move, preferred_element_type=F32
        )
    out[:32, :] = maps
    out[32:48, :] = bins


def loss_kernel(
    place, own, near, far, features, taps, probe, loss_out, map_grad, parts, token_grad
):
    seq, tile = place[0], place[1]
    own_rows = row_weights(seq, seq)
    depth = jnp.zeros((32, 256), F32)
    bins = jnp.zeros((32, 256), F32)
    for block, source in ((own, seq), (near, place[2]), (far, place[4])):
        depth = depth + dot(row_weights(seq, source), block[:32, :])
        move = pick(
            (32, 16),
            lambda i: (i >> 4) * 1024 + seq * 8 - 3 + (i & 15),
            lambda j: (j >> 3) * 1024 + source * 8 + (j & 7),
        )
        bins = bins + jnp.dot(move, block[32:48, :].astype(BF16), preferred_element_type=F32)
    target = (bins + 0.5) * (4.0 / NBINS) - 2.0
    error = depth - target
    loss = error * error
    for f in range(2):
        loss_out[f] = loss[f * 16 + 3 : f * 16 + 11, 3:163]
    y = lax.broadcasted_iota(jnp.int32, (32, 256), 0) & 15
    x = lax.broadcasted_iota(jnp.int32, (32, 256), 1)
    row = seq * 8 - 3 + y
    col = tile * 160 - 3 + x
    valid = (y < 14) & (x < 166) & (row >= 0) & (row < FULL_ROWS) & (col >= 0) & (col < FULL_COLS)
    grad = jnp.where(valid, 2.0 * error, 0.0)
    narrow = dot(own_rows, grad, TN)
    narrow = dot(narrow, col_weights(tile, tile), NT)
    for g in range(4):
        for b in range(3):
            token_grad[b * 8 : (b + 1) * 8, g * COLS : (g + 1) * COLS] = narrow[
                g * 8 : (g + 1) * 8, b * 128 : b * 128 + COLS
            ]
    grads = token_grad[...]
    map_grad[...] = dot(grads, taps[...], TN).astype(BF16)
    high, low = halves(grads)
    feature_grad = jnp.dot(high, features[...], preferred_element_type=F32) + jnp.dot(
        low, features[...], preferred_element_type=F32
    )
    high, low = halves(feature_grad)
    refine = jnp.dot(high, probe[...], preferred_element_type=F32) + jnp.dot(
        low, probe[...], preferred_element_type=F32
    )
    parts[...] = jnp.zeros_like(parts)
    for j in range(16):
        parts[j, :, :P_SIZE] = refine
        parts[j, :, P_SIZE : P_SIZE + 72] = feature_grad[:, j * 72 : (j + 1) * 72]


def plane_sum_kernel(parts, out):
    total = jnp.sum(parts[...], axis=0)
    out[...] = jnp.zeros_like(out)
    for z in range(8):
        out[z, :, :P_SIZE] = total[:, :P_SIZE]
        out[z, :, P_SIZE : P_SIZE + 9] = total[:, P_SIZE + z * 9 : P_SIZE + (z + 1) * 9]


def adam_step(grad, moment, second):
    new_moment = BETA_ONE * moment + (1.0 - BETA_ONE) * grad
    new_second = BETA_TWO * second + (1.0 - BETA_TWO) * grad * grad
    return (
        new_moment
        / (1.0 - BETA_ONE**STEP)
        / (jnp.sqrt(new_second / (1.0 - BETA_TWO**STEP)) + ADAM_EPS)
    )


def step_kernel(parts, taps, mom_probe, var_probe, mom_refine, var_refine, probe_out, refine_out):
    total = jnp.sum(parts[...], axis=0)
    probe_grad = dot(total[:, P_SIZE:], taps[...], TN)
    probe_out[...] = adam_step(probe_grad[:9], mom_probe[...], var_probe[...])
    for a in range(3):
        for b in range(3):
            refine_out[a, b : b + 1] = adam_step(
                total[b * 8 + a : b * 8 + a + 1, :P_SIZE],
                mom_refine[a, b : b + 1],
                var_refine[a, b : b + 1],
            )


def body(
    query_act,
    key_act,
    value_act,
    residual,
    gate_scale,
    w_out,
    w_probe,
    w_refine,
    depth_bins,
    mom_probe,
    var_probe,
    mom_refine,
    var_refine,
):
    seq = lax.axis_index(SEQ)
    tile = lax.axis_index(TILE)
    odd_seq = seq & 1
    odd_tile = tile & 1
    far_seq = seq + 2 * odd_seq - 1
    far_tile = tile + 2 * odd_tile - 1
    place = jnp.stack([seq, tile, seq ^ 1, tile ^ 1, far_seq, far_tile]).astype(jnp.int32)

    taps = jnp.pad(w_refine.transpose(1, 0, 2), ((0, 0), (0, 5), (0, 0))).reshape(24, P_SIZE)
    probe, tap_weights = call(
        weights_kernel,
        [jax.ShapeDtypeStruct((D, P_SIZE), BF16), jax.ShapeDtypeStruct((48, D), BF16)],
        (w_probe, taps),
        limit=16,
    )

    def split(act):
        return act.reshape(SEQ_COUNT, 1, 2, COLS * HD)

    sent = jnp.concatenate([split(query_act), split(key_act), split(value_act)], axis=1)
    here = lax.all_to_all(sent, SEQ, split_axis=0, concat_axis=0, tiled=True)
    queries = here[:, 0].reshape(ROWS, COLS * HD)
    own_kv = jnp.stack([here[:, i].reshape(ROWS, COLS * HD) for i in (1, 2)])
    swap_core = [(0, 1), (1, 0)]
    z_kv = lax.ppermute(own_kv, "z_hi", swap_core)
    core_kv = lax.ppermute(own_kv, "core", swap_core)
    query_rows, acc = attend(True, False, queries, own_kv)
    acc = attend(False, False, query_rows, core_kv, acc)
    z_core_kv = lax.ppermute(z_kv, "core", swap_core)
    acc = attend(False, False, query_rows, z_kv, acc)
    attended = attend(False, True, query_rows, z_core_kv, acc)
    merged = lax.all_to_all(
        attended.reshape(SEQ_COUNT, 2, COLS * HD), SEQ, split_axis=0, concat_axis=0, tiled=True
    ).reshape(ROWS, COLS * HD)

    features, tap_maps = call(
        features_kernel,
        [jax.ShapeDtypeStruct((160, D), BF16), jax.ShapeDtypeStruct((48, 384), F32)],
        (merged, residual.reshape(160, D), gate_scale.reshape(1, D), w_out, tap_weights, depth_bins.reshape(16, 160)),
        [pltpu.VMEM((TOKENS, 128), F32), pltpu.VMEM((160, D), F32)],
        limit=32,
    )
    tile_far = [(1, 2), (2, 1)]
    seq_near = [(i, i ^ 1) for i in range(SEQ_COUNT)]
    seq_far = [(i, i + 2 * (i & 1) - 1) for i in range(1, SEQ_COUNT - 1)]
    wide = call(
        widen_kernel,
        jax.ShapeDtypeStruct((48, 256), F32),
        (
            place,
            tap_maps,
            lax.ppermute(tap_maps, "core", swap_core),
            lax.ppermute(tap_maps, TILE, tile_far),
        ),
        limit=16,
    )
    loss_map, map_grad, parts = call(
        loss_kernel,
        [
            jax.ShapeDtypeStruct((2, 8, 160), F32),
            jax.ShapeDtypeStruct((160, P_SIZE), BF16),
            jax.ShapeDtypeStruct((16, 24, 384), F32),
        ],
        (
            place,
            wide,
            lax.ppermute(wide, SEQ, seq_near),
            lax.ppermute(wide, SEQ, seq_far),
            features,
            taps,
            probe,
        ),
        [pltpu.VMEM((24, 160), F32)],
        limit=16,
    )
    parts = lax.all_to_all(parts, PLANE, split_axis=0, concat_axis=0, tiled=True)
    parts = call(plane_sum_kernel, jax.ShapeDtypeStruct((8, 24, 384), F32), (parts,), limit=16)
    parts = lax.all_to_all(parts, COLUMN, split_axis=0, concat_axis=0, tiled=True)
    probe_step, refine_step = call(
        step_kernel,
        [
            jax.ShapeDtypeStruct((9, P_SIZE), F32),
            jax.ShapeDtypeStruct((3, 3, P_SIZE), F32),
        ],
        (parts, taps, mom_probe, var_probe, mom_refine, var_refine),
        limit=16,
    )
    return (loss_map, map_grad.reshape(2, 2, COLS, P_SIZE), probe_step, refine_step)


def solution(mesh):
    fine = Mesh(mesh.devices.reshape(4, 4, 2, 2, 2), ("y", "x", "z_lo", "z_hi", "core"))
    slab = (*SEQ, *TILE)
    in_specs = (
        P(None, None, SEQ, TILE),
        P(None, None, SEQ, TILE),
        P(None, None, SEQ, TILE),
        P(None, SEQ, TILE, None),
        P(),
        P(),
        P(),
        P(),
        P(None, SEQ, TILE),
        P(slab, None),
        P(slab, None),
        P(),
        P(),
    )
    out_specs = (
        P(None, SEQ, TILE),
        P(None, SEQ, TILE, None),
        P(slab, None),
        P(),
    )
    return jax.shard_map(body, mesh=fine, in_specs=in_specs, out_specs=out_specs, check_vma=False)
```

time: 535 us -> 168 us (0.31); the launches traced: 526 us -> 167 us
  waiting for transfers between devices: 138 us -> 12.7 us
  matrix products: 102 us -> 0 us
  local copies, waits for them, and re-layouts: 80.7 us -> 13.1 us
  Pallas kernels: 0 us -> 60.3 us
  blocking collectives: 102 us -> 57.6 us
  other arithmetic: 41.8 us -> 2.73 us
  starting transfers between devices: 46.2 us -> 20.1 us
  between operations: 14.8 us -> 0.87 us
    dot_general x28 -> x0, matrix products: 102 us -> none  [the longest x5 45.6 us: advance(): jnp.einsum('nqk,nkd->nqd', shifted.astype(jnp.bfloat16), value_slab, pref...]
    psum x1 -> x0, waiting for transfers between devices: 79.6 us -> none  [body(): lax.psum((probe_part, refine_part), ('seq', 'tile'))]
    psum x1 -> x0, blocking collectives: 70.1 us -> none  [body(): lax.psum((probe_part, refine_part), ('seq', 'tile'))]
    pallas_call x0 -> x10, Pallas kernels: none -> 60.3 us  [call(): pl.pallas_call(kernel, out_shape=out_shape, in_specs=in_specs, out_specs=...]
    all_gather x2 -> x0, waiting for transfers between devices: 49.2 us -> none  [the longest x1 28.2 us: body(): value_part = lax.all_gather(value_loc, 'tile', axis=3, tiled=True)]
    all_to_all x2 -> x3, blocking collectives: 31.7 us -> 57.6 us  [the longest x1 26.5 us: body(): here = lax.all_to_all(sent, SEQ, split_axis=0, concat_axis=0, tiled=True)]
    all_gather x2 -> x0, local copies, waits for them, and re-layouts: 23.9 us -> none  [the longest x1 12 us: body(): key_part = lax.all_gather(key_loc, 'tile', axis=3, tiled=True)]
    reshape x5 -> x4, local copies, waits for them, and re-layouts: 24.5 us -> 3.21 us  [the longest x1 1.93 us: body(): attended.reshape(SEQ_COUNT, 2, COLS * HD)]
  transfers between devices with their start and end apart: 13 -> 8, of which waited for: 6 -> 3; matrix products, arithmetic and copies ran while one was open for 8% -> 1% of each run, Pallas kernels for 0% -> 23%
where the time goes in v1:
time: 168 us; the launch traced here: 167 us
  Pallas kernels  60.3 us (36%)
  blocking collectives  57.6 us (34%)
  starting transfers between devices  20.1 us (12%)
  local copies, waits for them, and re-layouts  13.1 us (8%)
  waiting for transfers between devices  12.7 us (8%)
  other arithmetic  2.73 us (2%)
    pallas_call x10, Pallas kernels, call(): pl.pallas_call(kernel, out_shape=out_shape, in_specs=in_specs, out_specs=...  60.3 us
    all_to_all x1, blocking collectives, body(): here = lax.all_to_all(sent, SEQ, split_axis=0, concat_axis=0, tiled=True)  26.5 us
    all_to_all x1, blocking collectives, body(): lax.all_to_all(parts, PLANE, split_axis=0, concat_axis=0, tiled=True)  16.9 us
    all_to_all x1, blocking collectives, body(): lax.all_to_all(parts, COLUMN, split_axis=0, concat_axis=0, tiled=True)  14.2 us
    all_to_all x1, waiting for transfers between devices, body(): lax.all_to_all(attended.reshape(SEQ_COUNT, 2, COLS * HD), SEQ, split_axis...  7.86 us
    unnamed x38, local copies, waits for them, and re-layouts  7.39 us
    ppermute x1, starting transfers between devices, body(): lax.ppermute(tap_maps, TILE, tile_far)  5.13 us
    all_to_all x1, starting transfers between devices, body(): lax.all_to_all(attended.reshape(SEQ_COUNT, 2, COLS * HD), SEQ, split_axis...  4.85 us
  transfers between devices with their start and end apart: 8, of which 3 were waited for; matrix products, arithmetic and copies ran while one was open for 1% of the time, Pallas kernels for 23%

profile of v1, /device:TPU:1, one launch (start us, length us, event | category | flops | bytes accessed | tf_op | source)
XLA Modules:
  0.0 167.4 jit_solution(9068864451843533044)
XLA Ops:
  0.6 2.7 %pad_maximum_fusion = bf16[32,3,2,2880]{3,2,1,0:T(2,128)(2,1)S(1)} fusion(bf16[32,1,2,2880]{3,2,1,0:T(2,128)(2,1)} %bitcast.17, bf16[32,1,2,2880]{3,2,1,0:T(2,128)(2,1)} %bitcast.18, bf16[32,1,2,2880]{3,2,1,0:T(2,128)(2,1)} %bitcast.19), kind=kLoop, calls=%fused_computation | loop fusion | flops 1105920 | bytes 2211840 | tf_op jit(solution)/shard_map/concatenate | solution.py:366
  3.4 26.5 %all_to_all.20 = bf16[32,3,2,2880]{3,2,1,0:T(2,128)(2,1)S(1)} all-to-all(bf16[32,3,2,2880]{3,2,1,0:T(2,128)(2,1)S(1)} %pad_maximum_fusion), channel_id=1, replica_groups=mesh['y'=4,'x'=4,'z_lo'=2,'z_hi'=2,'core'=2] {'y','x','z_lo'}, dimensions={0} | all-to-all | bytes 2211840 | tf_op jit(solution)/shard_map/all_to_all | solution.py:367
  31.3 3.4 %collective-permute-start = (bf16[2,64,2880]{2,1,0:T(8,128)(2,1)S(1)}, bf16[2,64,2880]{2,1,0:T(8,128)(2,1)S(1)}, u32[]{:S(2)}, u32[]{:S(2)}) collective-permute-start(bf16[2,64,2880]{2,1,0:T(8,128)(2,1)S(1)} %constant_dynamic-update-slice_fusion.refs_1_), channel_id=1, source_target_pairs={{0,2},{2,0},{1,3},{3,1},{4,6},{6,4},{5,7},{7,5},{8,10},{10,8},{9,1... | collective-permute-start | bytes 2211848 | tf_op jit(solution)/shard_map/ppermute | solution.py:371
  34.7 2.4 %collective-permute-start.2 = (bf16[2,64,2880]{2,1,0:T(8,128)(2,1)S(1)}, bf16[2,64,2880]{2,1,0:T(8,128)(2,1)S(1)}, u32[]{:S(2)}, u32[]{:S(2)}) collective-permute-start(bf16[2,64,2880]{2,1,0:T(8,128)(2,1)S(1)} %constant_dynamic-update-slice_fusion.refs_1_), channel_id=1, source_target_pairs={{0,1},{1,0},{2,3},{3,2},{4,5},{5,4},{6,7},{7,6},{8,9},{9,8},{10,11... | collective-permute-start | bytes 2211848 | tf_op jit(solution)/shard_map/ppermute | solution.py:372
  38.2 12.0 %shard_map.156 = (bf16[2560,128]{1,0:T(8,128)(2,1)}, f32[2560,128]{1,0:T(8,128)}) custom-call(bf16[64,2880]{1,0:T(8,128)(2,1)} %reshape_squeeze.3.refs_0_, bf16[2,64,2880]{2,1,0:T(8,128)(2,1)} %copy-done.12), custom_call_target="tpu_custom_call" | custom-call | flops 6710886400 | bytes 4194304 | tf_op jit(solution)/shard_map/pallas_call | solution.py:49
  50.2 2.3 %collective-permute-start.1 = (bf16[2,64,2880]{2,1,0:T(8,128)(2,1)S(1)}, bf16[2,64,2880]{2,1,0:T(8,128)(2,1)S(1)}, u32[]{:S(2)}, u32[]{:S(2)}) collective-permute-start(bf16[2,64,2880]{2,1,0:T(8,128)(2,1)S(1)} %collective-permute-done.refs_1_), channel_id=1, source_target_pairs={{0,1},{1,0},{2,3},{3,2},{4,5},{5,4},{6,7},{7,6},{8,9},{9,8},{10,11... | collective-permute-start | bytes 2211848 | tf_op jit(solution)/shard_map/ppermute | solution.py:375
  53.4 13.1 %shard_map.157.refs_2_ = f32[2560,128]{1,0:T(8,128)} custom-call(bf16[2560,128]{1,0:T(8,128)(2,1)} %get-tuple-element.15.refs_0_, bf16[2,64,2880]{2,1,0:T(8,128)(2,1)} %copy-done.16, f32[2560,128]{1,0:T(8,128)} %get-tuple-element.16.refs_2_), custom_call_target="tpu_custom_call" | custom-call | flops 6710886400 | bytes 4194304 | tf_op jit(solution)/shard_map/pallas_call | solution.py:49
  66.5 13.1 %shard_map.158.refs_2_ = f32[2560,128]{1,0:T(8,128)} custom-call(bf16[2560,128]{1,0:T(8,128)(2,1)} %get-tuple-element.15.refs_0_, bf16[2,64,2880]{2,1,0:T(8,128)(2,1)} %copy-done.15, f32[2560,128]{1,0:T(8,128)} %shard_map.157.refs_2_), custom_call_target="tpu_custom_call" | custom-call | flops 6710886400 | bytes 4194304 | tf_op jit(solution)/shard_map/pallas_call | solution.py:49
  80.4 13.6 %shard_map.159 = bf16[64,2880]{1,0:T(8,128)(2,1)} custom-call(bf16[2560,128]{1,0:T(8,128)(2,1)} %get-tuple-element.15.refs_0_, bf16[2,64,2880]{2,1,0:T(8,128)(2,1)} %copy-done.17, f32[2560,128]{1,0:T(8,128)} %shard_map.158.refs_2_), custom_call_target="tpu_custom_call" | custom-call | flops 6710886400 | bytes 4194304 | tf_op jit(solution)/shard_map/pallas_call | solution.py:49
  94.0 1.9 %reshape.41 = bf16[32,2,2880]{2,1,0:T(2,128)(2,1)} reshape(bf16[64,2880]{1,0:T(8,128)(2,1)} %shard_map.159) | data formatting | bytes 737280 | tf_op jit(solution)/shard_map/reshape | solution.py:379
  96.0 4.9 %all-to-all-start.1 = ((bf16[32,2,2880]{2,1,0:T(2,128)(2,1)}), bf16[32,2,2880]{2,1,0:T(2,128)(2,1)}, u32[]{:S(2)}, u32[]{:S(2)}) async-start(bf16[32,2,2880]{2,1,0:T(2,128)(2,1)} %reshape.41), calls=%async_computation.1 | async-start | bytes 753664 | tf_op jit(solution)/shard_map/all_to_all | solution.py:378
  100.9 1.3 copy-done.1
  103.3 7.9 %all-to-all-done.1 = bf16[32,2,2880]{2,1,0:T(2,128)(2,1)} async-done(((bf16[32,2,2880]{2,1,0:T(2,128)(2,1)}), bf16[32,2,2880]{2,1,0:T(2,128)(2,1)}, u32[]{:S(2)}, u32[]{:S(2)}) %all-to-all-start.1) | async-done | bytes 368672 | tf_op jit(solution)/shard_map/all_to_all | solution.py:378
  111.2 1.3 reshape.42.merged
  113.2 2.8 %shard_map.161 = (bf16[160,1152]{1,0:T(8,128)(2,1)S(1)}, f32[48,384]{1,0:T(8,128)}) custom-call(bf16[64,2880]{1,0:T(8,128)(2,1)S(1)} %reshape.42.merged, bf16[160,1152]{1,0:T(8,128)(2,1)S(1)} %bitcast.15, f32[1,1152]{1,0:T(1,128)S(1)} %reshape.44.gate, bf16[1152,1152]{1,0:T(8,128)(2,1)S(1)} %copy-done, bf16[48,1152]{1,0:T(8,128)(2,1)S(1)} %get-tuple-element.17.tap_weights, ...), custom_call_target="tpu_custom_call" | custom-call | tf_op jit(solution)/shard_map/pallas_call | solution.py:49
  116.8 1.2 collective-permute-start.3
  118.0 5.1 %collective-permute-start.4 = (f32[48,384]{1,0:T(8,128)}, f32[48,384]{1,0:T(8,128)S(1)}, u32[]{:S(2)}, u32[]{:S(2)}) collective-permute-start(f32[48,384]{1,0:T(8,128)} %get-tuple-element.18.own), channel_id=1, source_target_pairs={{1,2},{2,1},{5,6},{6,5},{9,10},{10,9},{13,14},{14,13},{17,18},{18,... | collective-permute-start | bytes 221192 | tf_op jit(solution)/shard_map/ppermute | solution.py:399
  123.2 2.6 %collective-permute-done.4.far = f32[48,384]{1,0:T(8,128)S(1)} collective-permute-done((f32[48,384]{1,0:T(8,128)}, f32[48,384]{1,0:T(8,128)S(1)}, u32[]{:S(2)}, u32[]{:S(2)}) %collective-permute-start.4) | collective-permute-done | bytes 73760 | tf_op jit(solution)/shard_map/ppermute | solution.py:399
  125.9 1.6 shard_map.162.own
  128.2 2.3 %collective-permute-done.5.near = f32[48,256]{1,0:T(8,128)S(1)} collective-permute-done((f32[48,256]{1,0:T(8,128)S(1)}, f32[48,256]{1,0:T(8,128)S(1)}, u32[]{:S(2)}, u32[]{:S(2)}) %collective-permute-start.5) | collective-permute-done | bytes 49184 | tf_op jit(solution)/shard_map/ppermute | solution.py:413
  130.5 1.1 copy-done.3
  132.5 2.7 %shard_map.163 = (f32[2,8,160]{2,1,0:T(8,128)}, bf16[160,256]{1,0:T(8,128)(2,1)}, f32[16,24,384]{2,1,0:T(8,128)S(1)}) custom-call(s32[6]{0:T(128)S(1)} %stack.30.place, f32[48,256]{1,0:T(8,128)S(1)} %shard_map.162.own, f32[48,256]{1,0:T(8,128)S(1)} %collective-permute-done.5.near, f32[48,256]{1,0:T(8,128)S(1)} %collective-permute-done.6.far, ...), custom_call_target="tpu_custom_call" | custom-call | tf_op jit(solution)/shard_map/pallas_call | solution.py:49
  135.2 16.9 %all_to_all.21.parts = f32[16,24,384]{2,1,0:T(8,128)S(1)} all-to-all(f32[16,24,384]{2,1,0:T(8,128)S(1)} %get-tuple-element.23), channel_id=1, replica_groups=mesh['y'=4,'x'=4,'z_lo'=2,'z_hi'=2,'core'=2] {'y','x'}, dimensions={0} | all-to-all | bytes 1179648 | tf_op jit(solution)/shard_map/all_to_all | solution.py:422
  152.3 14.2 %all_to_all.22.parts = f32[8,24,384]{2,1,0:T(8,128)S(1)} all-to-all(f32[8,24,384]{2,1,0:T(8,128)S(1)} %shard_map.164), channel_id=1, replica_groups=mesh['y'=4,'x'=4,'z_lo'=2,'z_hi'=2,'core'=2] {'z_lo','z_hi','core'}, dimensions={0} | all-to-all | bytes 589824 | tf_op jit(solution)/shard_map/all_to_all | solution.py:424
  (54 shorter events, 9.7 us)
Async XLA Ops:
  31.3 6.9 %copy-start.12 = (bf16[2,64,2880]{2,1,0:T(8,128)(2,1)}, bf16[2,64,2880]{2,1,0:T(8,128)(2,1)S(1)}, u32[]{:S(2)}) copy-start(bf16[2,64,2880]{2,1,0:T(8,128)(2,1)S(1)} %constant_dynamic-update-slice_fusion.refs_1_) | copy-start | bytes 2211844
  31.3 18.9 %collective-permute-start = (bf16[2,64,2880]{2,1,0:T(8,128)(2,1)S(1)}, bf16[2,64,2880]{2,1,0:T(8,128)(2,1)S(1)}, u32[]{:S(2)}, u32[]{:S(2)}) collective-permute-start(bf16[2,64,2880]{2,1,0:T(8,128)(2,1)S(1)} %constant_dynamic-update-slice_fusion.refs_1_), channel_id=1, source_target_pairs={{0,2},{2,0},{1,3},{3,1},{4,6},{6,4},{5,7},{7,5},{8,10},{10,8},{9,1... | collective-permute-start | bytes 2211848 | tf_op jit(solution)/shard_map/ppermute | solution.py:371
  34.7 17.8 %collective-permute-start.2 = (bf16[2,64,2880]{2,1,0:T(8,128)(2,1)S(1)}, bf16[2,64,2880]{2,1,0:T(8,128)(2,1)S(1)}, u32[]{:S(2)}, u32[]{:S(2)}) collective-permute-start(bf16[2,64,2880]{2,1,0:T(8,128)(2,1)S(1)} %constant_dynamic-update-slice_fusion.refs_1_), channel_id=1, source_target_pairs={{0,1},{1,0},{2,3},{3,2},{4,5},{5,4},{6,7},{7,6},{8,9},{9,8},{10,11... | collective-permute-start | bytes 2211848 | tf_op jit(solution)/shard_map/ppermute | solution.py:372
  50.2 16.2 %copy-start.15 = (bf16[2,64,2880]{2,1,0:T(8,128)(2,1)}, bf16[2,64,2880]{2,1,0:T(8,128)(2,1)S(1)}, u32[]{:S(2)}) copy-start(bf16[2,64,2880]{2,1,0:T(8,128)(2,1)S(1)} %collective-permute-done.refs_1_) | copy-start | bytes 2211844
  50.2 29.3 %collective-permute-start.1 = (bf16[2,64,2880]{2,1,0:T(8,128)(2,1)S(1)}, bf16[2,64,2880]{2,1,0:T(8,128)(2,1)S(1)}, u32[]{:S(2)}, u32[]{:S(2)}) collective-permute-start(bf16[2,64,2880]{2,1,0:T(8,128)(2,1)S(1)} %collective-permute-done.refs_1_), channel_id=1, source_target_pairs={{0,1},{1,0},{2,3},{3,2},{4,5},{5,4},{6,7},{7,6},{8,9},{9,8},{10,11... | collective-permute-start | bytes 2211848 | tf_op jit(solution)/shard_map/ppermute | solution.py:375
  52.5 0.9 copy-start.16
  79.5 0.9 copy-start.17
  94.0 6.8 %copy-start.13 = (f32[3,3,256]{2,1,0:T(4,128)S(1)}, f32[3,3,256]{2,1,0:T(4,128)}, u32[]{:S(2)}) copy-start(f32[3,3,256]{2,1,0:T(4,128)} %param.20) | copy-start | bytes 27652
  94.0 6.8 %copy-start.14 = (f32[1152]{0:T(1024)S(1)}, f32[1152]{0:T(1024)}, u32[]{:S(2)}) copy-start(f32[1152]{0:T(1024)} %param.17) | copy-start | bytes 13828
  94.0 18.4 %copy-start.4 = (bf16[2,2,40,1152]{3,2,1,0:T(8,128)(2,1)S(1)}, bf16[2,2,40,1152]{3,2,1,0:T(8,128)(2,1)}, u32[]{:S(2)}) copy-start(bf16[2,2,40,1152]{3,2,1,0:T(8,128)(2,1)} %param.16) | copy-start | bytes 1105924
  96.0 16.5 %copy-start = (bf16[1152,1152]{1,0:T(8,128)(2,1)S(1)}, bf16[1152,1152]{1,0:T(8,128)(2,1)}, u32[]{:S(2)}) copy-start(bf16[1152,1152]{1,0:T(8,128)(2,1)} %w_out.1) | copy-start | bytes 7962628
  96.0 15.2 %all-to-all-start.1 = ((bf16[32,2,2880]{2,1,0:T(2,128)(2,1)}), bf16[32,2,2880]{2,1,0:T(2,128)(2,1)}, u32[]{:S(2)}, u32[]{:S(2)}) async-start(bf16[32,2,2880]{2,1,0:T(2,128)(2,1)} %reshape.41), calls=%async_computation.1 | async-start | bytes 753664 | tf_op jit(solution)/shard_map/all_to_all | solution.py:378
  100.9 1.3 copy-start.1
  102.5 0.8 copy-start.2
  116.8 6.5 %collective-permute-start.3 = (f32[48,384]{1,0:T(8,128)}, f32[48,384]{1,0:T(8,128)S(1)}, u32[]{:S(2)}, u32[]{:S(2)}) collective-permute-start(f32[48,384]{1,0:T(8,128)} %get-tuple-element.18.own), channel_id=1, source_target_pairs={{0,1},{1,0},{2,3},{3,2},{4,5},{5,4},{6,7},{7,6},{8,9},{9,8},{10,11... | collective-permute-start | bytes 221192 | tf_op jit(solution)/shard_map/ppermute | solution.py:398
  118.0 7.9 %collective-permute-start.4 = (f32[48,384]{1,0:T(8,128)}, f32[48,384]{1,0:T(8,128)S(1)}, u32[]{:S(2)}, u32[]{:S(2)}) collective-permute-start(f32[48,384]{1,0:T(8,128)} %get-tuple-element.18.own), channel_id=1, source_target_pairs={{1,2},{2,1},{5,6},{6,5},{9,10},{10,9},{13,14},{14,13},{17,18},{18,... | collective-permute-start | bytes 221192 | tf_op jit(solution)/shard_map/ppermute | solution.py:399
  127.4 3.0 %collective-permute-start.5 = (f32[48,256]{1,0:T(8,128)S(1)}, f32[48,256]{1,0:T(8,128)S(1)}, u32[]{:S(2)}, u32[]{:S(2)}) collective-permute-start(f32[48,256]{1,0:T(8,128)S(1)} %shard_map.162.own), channel_id=1, source_target_pairs={{0,4},{4,0},{8,12},{12,8},{16,20},{20,16},{24,28},{28,24},{32,36},... | collective-permute-start | bytes 147464 | tf_op jit(solution)/shard_map/ppermute | solution.py:413
  127.5 2.9 %collective-permute-start.6 = (f32[48,256]{1,0:T(8,128)S(1)}, f32[48,256]{1,0:T(8,128)S(1)}, u32[]{:S(2)}, u32[]{:S(2)}) collective-permute-start(f32[48,256]{1,0:T(8,128)S(1)} %shard_map.162.own), channel_id=1, source_target_pairs={{4,8},{8,4},{12,16},{16,12},{20,24},{24,20},{28,32},{32,28},{36,40... | collective-permute-start | bytes 147464 | tf_op jit(solution)/shard_map/ppermute | solution.py:414
  130.4 1.1 copy-start.3
  131.5 1.0 copy-start.6
  135.2 31.2 %copy-start.7 = (f32[9,256]{1,0:T(8,128)S(1)}, f32[9,256]{1,0:T(8,128)}, u32[]{:S(2)}) copy-start(f32[9,256]{1,0:T(8,128)} %mom_probe.1) | copy-start | bytes 27652
  135.2 31.2 %copy-start.8 = (f32[9,256]{1,0:T(8,128)S(1)}, f32[9,256]{1,0:T(8,128)}, u32[]{:S(2)}) copy-start(f32[9,256]{1,0:T(8,128)} %var_probe.1) | copy-start | bytes 27652
  135.2 31.2 %copy-start.10 = (f32[3,3,256]{2,1,0:T(4,128)S(1)}, f32[3,3,256]{2,1,0:T(4,128)}, u32[]{:S(2)}) copy-start(f32[3,3,256]{2,1,0:T(4,128)} %mom_refine.1) | copy-start | bytes 27652
  135.2 31.2 %copy-start.11 = (f32[3,3,256]{2,1,0:T(4,128)S(1)}, f32[3,3,256]{2,1,0:T(4,128)}, u32[]{:S(2)}) copy-start(f32[3,3,256]{2,1,0:T(4,128)} %var_refine.1) | copy-start | bytes 27652
  (2 other events, 1.5 us)

commit v2 on v1

--- a/solution.py
+++ b/solution.py
@@ -17,7 +17,7 @@
 ROWS = 64
 COLS = 40
 TOKENS = ROWS * COLS
-BLOCK = 256
+BLOCK = 512
 SEQ_COUNT = 32
 TILE_COUNT = 4
 FULL_ROWS = 256
@@ -43,8 +43,20 @@
 SMEM = pl.BlockSpec(memory_space=pltpu.SMEM)
 
 
-def call(kernel, out_shape, operands, scratch=(), flops=0, bytes_accessed=0, transcendentals=0, limit=56):
+def call(
+    kernel,
+    out_shape,
+    operands,
+    scratch=(),
+    flops=0,
+    bytes_accessed=0,
+    transcendentals=0,
+    limit=56,
+    left=0,
+):
     in_specs = [SMEM if x.dtype == jnp.int32 and x.ndim == 1 else VMEM for x in operands]
+    for i in range(len(operands) - left, len(operands)):
+        in_specs[i] = pl.BlockSpec(memory_space=pl.ANY)
     many = isinstance(out_shape, (list, tuple))
     return pl.pallas_call(
         kernel,
@@ -84,17 +96,18 @@
     value_rows[...] = jnp.where(lane == HD, 1.0, 0.0).astype(BF16)
     unpack(kv_ref.at[0], key_rows)
     unpack(kv_ref.at[1], value_rows)
-    blocks = TOKENS // BLOCK
-    block_lane = lax.broadcasted_iota(jnp.int32, (BLOCK, 128), 1)
-
-    def scores(i):
-        rows = pl.ds(pl.multiple_of(i * BLOCK, BLOCK), BLOCK)
-        return lax.dot_general(query_rows[rows, :], key_rows[...], NT, preferred_element_type=F32)
-
-    def step(i, now, later):
-        scores_ref[later] = scores(jnp.minimum(i + 1, blocks - 1))
-        rows = pl.ds(pl.multiple_of(i * BLOCK, BLOCK), BLOCK)
-        block = scores_ref[now]
+
+    def block_rows(i):
+        return pl.ds(pl.multiple_of(i * BLOCK, BLOCK), BLOCK)
+
+    def scores(i, slot):
+        scores_ref[slot] = lax.dot_general(
+            query_rows[block_rows(i), :], key_rows[...], NT, preferred_element_type=F32
+        )
+
+    def finish(i, slot):
+        rows = block_rows(i)
+        block = scores_ref[slot]
         top = jnp.max(block, axis=1, keepdims=True)
         if not first:
             old = acc_ref[rows, :]
@@ -107,16 +120,19 @@
         if last:
             acc_out[rows, :] = total / total[:, HD : HD + 1]
         else:
+            block_lane = lax.broadcasted_iota(jnp.int32, (BLOCK, 128), 1)
             acc_out[rows, :] = jnp.where(block_lane == HD + 1, top, total)
 
-    scores_ref[0] = scores(0)
-
     def pair(j, carry):
-        step(2 * j, 0, 1)
-        step(2 * j + 1, 1, 0)
+        scores(2 * j + 1, 1)
+        finish(2 * j, 0)
+        scores(2 * j + 2, 0)
+        finish(2 * j + 1, 1)
         return carry
 
-    lax.fori_loop(0, blocks // 2, pair, 0)
+    scores(0, 0)
+    lax.fori_loop(0, TOKENS // BLOCK // 2, pair, 0)
+    finish(TOKENS // BLOCK - 1, 0)
     if last:
         for c in range(COLS):
             out_ref[:, c * HD : (c + 1) * HD] = acc_out[c * ROWS : (c + 1) * ROWS, :HD].astype(BF16)
@@ -146,10 +162,12 @@
         flops=4 * TOKENS * TOKENS * 256,
         bytes_accessed=4 * 2**20,
         transcendentals=TOKENS * TOKENS,
-    )
-
-
-def weights_kernel(w_probe, taps, probe_out, tap_weights):
+        limit=24,
+    )
+
+
+def weights_kernel(w_probe, taps, bins, probe_out, tap_weights, bins_out):
+    bins_out[...] = bins[...].astype(F32)
     probe = w_probe[...].astype(BF16)
     probe_out[...] = probe
     high, low = halves(taps[...])
@@ -186,7 +204,7 @@
             tap_maps[g * 8 : (g + 1) * 8, b * 128 : b * 128 + COLS] = maps[
                 b * 8 : (b + 1) * 8, g * COLS : (g + 1) * COLS
             ]
-    tap_maps[32:48, :160] = bins[...].astype(F32)
+    tap_maps[32:48, :160] = bins[...]
 
 
 def hat(offset):
@@ -210,7 +228,7 @@
     tap = i >> 7
     c = i & 127
     weight = interp(tile * 160 - 4 + x + tap, source * COLS + c, TILE_COUNT * COLS)
-    return jnp.where(c < COLS, weight, 0.0)
+    return jnp.where(c < COLS, weight, 0.0).astype(BF16)
 
 
 def row_weights(seq, source):
@@ -220,13 +238,23 @@
     y = i & 15
     tap = j & 7
     weight = interp(seq * 8 - 4 + y + tap, source * 2 + ((j >> 3) & 1), ROWS)
-    return jnp.where(((i >> 4) == (j >> 4)) & (tap < 3), weight, 0.0)
-
-
-def dot(left, right, dims=None):
-    if dims is None:
-        dims = (((1,), (0,)), ((), ()))
-    return lax.dot_general(left, right, dims, precision=PRECISE, preferred_element_type=F32)
+    return jnp.where(((i >> 4) == (j >> 4)) & (tap < 3), weight, 0.0).astype(BF16)
+
+
+def dot(left, right, dims=(((1,), (0,)), ((), ()))):
+    return lax.dot_general(left, right, dims, preferred_element_type=F32)
+
+
+def dot_left(left, weights, dims=(((1,), (0,)), ((), ()))):
+    both = dot(jnp.concatenate(halves(left), 0), weights, dims)
+    rows = left.shape[0]
+    return both[:rows] + both[rows:]
+
+
+def dot_right(weights, right, dims=(((1,), (0,)), ((), ()))):
+    both = dot(weights, jnp.concatenate(halves(right), 1), dims)
+    cols = right.shape[1]
+    return both[:, :cols] + both[:, cols:]
 
 
 def pick(shape, wanted, there):
@@ -235,35 +263,69 @@
     return jnp.where(wanted(i) == there(j), 1.0, 0.0).astype(BF16)
 
 
-def widen_kernel(place, own, near, far, out):
+def move_bins(block, tile, source):
+    move = pick((160, 256), lambda i: source * 160 + i, lambda j: tile * 160 - 3 + j)
+    return dot(block[32:48, :160].astype(BF16), move)
+
+
+def widen_own_kernel(place, own, out, own_cols, near_cols, far_cols):
     tile = place[1]
-    maps = jnp.zeros((32, 256), F32)
-    bins = jnp.zeros((16, 256), F32)
-    for block, source in ((own, tile), (near, place[3]), (far, place[5])):
-        maps = maps + dot(block[:32, :], col_weights(tile, source))
-        move = pick((160, 256), lambda i: source * 160 + i, lambda j: tile * 160 - 3 + j)
-        bins = bins + jnp.dot(
-            block[32:48, :160].astype(BF16), move, preferred_element_type=F32
-        )
-    out[:32, :] = maps
-    out[32:48, :] = bins
+    cols = col_weights(tile, tile)
+    out[:32, :] = dot_left(own[:32, :], cols)
+    out[32:48, :] = move_bins(own, tile, tile)
+    own_cols[...] = cols
+    near_cols[...] = col_weights(tile, place[3])
+    far_cols[...] = col_weights(tile, place[5])
+
+
+def widen_kernel(place, own, near, near_cols, far, far_cols, out):
+    tile = place[1]
+    out[:32, :] = (
+        own[:32, :]
+        + dot_left(near[:32, :], near_cols[...])
+        + dot_left(far[:32, :], far_cols[...])
+    )
+    out[32:48, :] = (
+        own[32:48, :] + move_bins(near, tile, place[3]) + move_bins(far, tile, place[5])
+    )
 
 
 def loss_kernel(
-    place, own, near, far, features, taps, probe, loss_out, map_grad, parts, token_grad
+    place,
+    own,
+    near,
+    far,
+    own_cols,
+    taps,
+    features_hbm,
+    probe_hbm,
+    loss_out,
+    map_grad,
+    parts,
+    token_grad,
+    nine,
+    features,
+    probe,
+    sems,
 ):
+    copies = [
+        pltpu.make_async_copy(features_hbm, features, sems.at[0]),
+        pltpu.make_async_copy(probe_hbm, probe, sems.at[1]),
+    ]
+    for copy in copies:
+        copy.start()
     seq, tile = place[0], place[1]
     own_rows = row_weights(seq, seq)
     depth = jnp.zeros((32, 256), F32)
     bins = jnp.zeros((32, 256), F32)
     for block, source in ((own, seq), (near, place[2]), (far, place[4])):
-        depth = depth + dot(row_weights(seq, source), block[:32, :])
+        depth = depth + dot_right(row_weights(seq, source), block[:32, :])
         move = pick(
             (32, 16),
             lambda i: (i >> 4) * 1024 + seq * 8 - 3 + (i & 15),
             lambda j: (j >> 3) * 1024 + source * 8 + (j & 7),
         )
-        bins = bins + jnp.dot(move, block[32:48, :].astype(BF16), preferred_element_type=F32)
+        bins = bins + dot(move, block[32:48, :].astype(BF16))
     target = (bins + 0.5) * (4.0 / NBINS) - 2.0
     error = depth - target
     loss = error * error
@@ -275,15 +337,18 @@
     col = tile * 160 - 3 + x
     valid = (y < 14) & (x < 166) & (row >= 0) & (row < FULL_ROWS) & (col >= 0) & (col < FULL_COLS)
     grad = jnp.where(valid, 2.0 * error, 0.0)
-    narrow = dot(own_rows, grad, TN)
-    narrow = dot(narrow, col_weights(tile, tile), NT)
+    narrow = dot_left(dot_right(own_rows, grad, TN), own_cols[...], NT)
     for g in range(4):
         for b in range(3):
             token_grad[b * 8 : (b + 1) * 8, g * COLS : (g + 1) * COLS] = narrow[
                 g * 8 : (g + 1) * 8, b * 128 : b * 128 + COLS
             ]
     grads = token_grad[...]
-    map_grad[...] = dot(grads, taps[...], TN).astype(BF16)
+    map_grad[...] = lax.dot_general(
+        grads, taps[...], TN, precision=PRECISE, preferred_element_type=F32
+    ).astype(BF16)
+    for copy in copies:
+        copy.wait()
     high, low = halves(grads)
     feature_grad = jnp.dot(high, features[...], preferred_element_type=F32) + jnp.dot(
         low, features[...], preferred_element_type=F32
@@ -292,18 +357,22 @@
     refine = jnp.dot(high, probe[...], preferred_element_type=F32) + jnp.dot(
         low, probe[...], preferred_element_type=F32
     )
-    parts[...] = jnp.zeros_like(parts)
+    nine[...] = jnp.zeros_like(nine)
+    for b in range(3):
+        nine[b * 3 : (b + 1) * 3, :P_SIZE] = refine[b * 8 : b * 8 + 3]
+        nine[b * 3 : (b + 1) * 3, P_SIZE:] = feature_grad[b * 8 : b * 8 + 3]
+    every = nine[:, :P_SIZE]
     for j in range(16):
-        parts[j, :, :P_SIZE] = refine
-        parts[j, :, P_SIZE : P_SIZE + 72] = feature_grad[:, j * 72 : (j + 1) * 72]
+        own = nine[:, P_SIZE + j * 72 : P_SIZE + (j + 1) * 72]
+        parts[j] = jnp.concatenate([every, own, jnp.zeros((16, 56), F32)], 1).astype(BF16)
 
 
 def plane_sum_kernel(parts, out):
-    total = jnp.sum(parts[...], axis=0)
-    out[...] = jnp.zeros_like(out)
+    total = jnp.sum(parts[...].astype(F32), axis=0)
+    every = total[:, :P_SIZE]
     for z in range(8):
-        out[z, :, :P_SIZE] = total[:, :P_SIZE]
-        out[z, :, P_SIZE : P_SIZE + 9] = total[:, P_SIZE + z * 9 : P_SIZE + (z + 1) * 9]
+        own = total[:, P_SIZE + z * 9 : P_SIZE + (z + 1) * 9]
+        out[z] = jnp.concatenate([every, own, jnp.zeros((16, 119), F32)], 1).astype(BF16)
 
 
 def adam_step(grad, moment, second):
@@ -316,17 +385,22 @@
     )
 
 
-def step_kernel(parts, taps, mom_probe, var_probe, mom_refine, var_refine, probe_out, refine_out):
-    total = jnp.sum(parts[...], axis=0)
-    probe_grad = dot(total[:, P_SIZE:], taps[...], TN)
-    probe_out[...] = adam_step(probe_grad[:9], mom_probe[...], var_probe[...])
+def step_kernel(
+    parts, w_refine, mom_probe, var_probe, mom_refine, var_refine, probe_out, refine_out, taps
+):
+    total = jnp.sum(parts[...].astype(F32), axis=0)
+    taps[...] = jnp.zeros_like(taps)
     for a in range(3):
         for b in range(3):
+            i = b * 3 + a
+            taps[i : i + 1] = w_refine[a, b : b + 1]
             refine_out[a, b : b + 1] = adam_step(
-                total[b * 8 + a : b * 8 + a + 1, :P_SIZE],
-                mom_refine[a, b : b + 1],
-                var_refine[a, b : b + 1],
+                total[i : i + 1, :P_SIZE], mom_refine[a, b : b + 1], var_refine[a, b : b + 1]
             )
+    probe_grad = lax.dot_general(
+        total[:, P_SIZE:], taps[...], TN, precision=PRECISE, preferred_element_type=F32
+    )
+    probe_out[...] = adam_step(probe_grad[:9], mom_probe[...], var_probe[...])
 
 
 def body(
@@ -353,10 +427,14 @@
     place = jnp.stack([seq, tile, seq ^ 1, tile ^ 1, far_seq, far_tile]).astype(jnp.int32)
 
     taps = jnp.pad(w_refine.transpose(1, 0, 2), ((0, 0), (0, 5), (0, 0))).reshape(24, P_SIZE)
-    probe, tap_weights = call(
+    probe, tap_weights, bins = call(
         weights_kernel,
-        [jax.ShapeDtypeStruct((D, P_SIZE), BF16), jax.ShapeDtypeStruct((48, D), BF16)],
-        (w_probe, taps),
+        [
+            jax.ShapeDtypeStruct((D, P_SIZE), BF16),
+            jax.ShapeDtypeStruct((48, D), BF16),
+            jax.ShapeDtypeStruct((16, 160), F32),
+        ],
+        (w_probe, taps, depth_bins.reshape(16, 160)),
         limit=16,
     )
 
@@ -371,7 +449,9 @@
     z_kv = lax.ppermute(own_kv, "z_hi", swap_core)
     core_kv = lax.ppermute(own_kv, "core", swap_core)
     query_rows, acc = attend(True, False, queries, own_kv)
+    acc, probe, tap_weights, bins = lax.optimization_barrier((acc, probe, tap_weights, bins))
     acc = attend(False, False, query_rows, core_kv, acc)
+    z_kv, acc = lax.optimization_barrier((z_kv, acc))
     z_core_kv = lax.ppermute(z_kv, "core", swap_core)
     acc = attend(False, False, query_rows, z_kv, acc)
     attended = attend(False, True, query_rows, z_core_kv, acc)
@@ -382,45 +462,57 @@
     features, tap_maps = call(
         features_kernel,
         [jax.ShapeDtypeStruct((160, D), BF16), jax.ShapeDtypeStruct((48, 384), F32)],
-        (merged, residual.reshape(160, D), gate_scale.reshape(1, D), w_out, tap_weights, depth_bins.reshape(16, 160)),
+        (
+            merged,
+            residual.reshape(160, D),
+            gate_scale.reshape(1, D),
+            w_out,
+            tap_weights,
+            bins,
+        ),
         [pltpu.VMEM((TOKENS, 128), F32), pltpu.VMEM((160, D), F32)],
         limit=32,
     )
     tile_far = [(1, 2), (2, 1)]
     seq_near = [(i, i ^ 1) for i in range(SEQ_COUNT)]
     seq_far = [(i, i + 2 * (i & 1) - 1) for i in range(1, SEQ_COUNT - 1)]
+    map_far = lax.ppermute(tap_maps, TILE, tile_far)
+    map_near = lax.ppermute(tap_maps, "core", swap_core)
+    cols = jax.ShapeDtypeStruct((384, 256), BF16)
+    wide, own_cols, near_cols, far_cols = call(
+        widen_own_kernel,
+        [jax.ShapeDtypeStruct((48, 256), F32), cols, cols, cols],
+        (place, tap_maps),
+        limit=16,
+    )
     wide = call(
         widen_kernel,
         jax.ShapeDtypeStruct((48, 256), F32),
-        (
-            place,
-            tap_maps,
-            lax.ppermute(tap_maps, "core", swap_core),
-            lax.ppermute(tap_maps, TILE, tile_far),
-        ),
+        (place, wide, map_near, near_cols, map_far, far_cols),
         limit=16,
     )
+    wide_far = lax.ppermute(wide, SEQ, seq_far)
+    wide_near = lax.ppermute(wide, SEQ, seq_near)
     loss_map, map_grad, parts = call(
         loss_kernel,
         [
             jax.ShapeDtypeStruct((2, 8, 160), F32),
             jax.ShapeDtypeStruct((160, P_SIZE), BF16),
-            jax.ShapeDtypeStruct((16, 24, 384), F32),
+            jax.ShapeDtypeStruct((16, 16, 384), BF16),
         ],
-        (
-            place,
-            wide,
-            lax.ppermute(wide, SEQ, seq_near),
-            lax.ppermute(wide, SEQ, seq_far),
-            features,
-            taps,
-            probe,
-        ),
-        [pltpu.VMEM((24, 160), F32)],
+        (place, wide, wide_near, wide_far, own_cols, taps, features, probe),
+        [
+            pltpu.VMEM((24, 160), F32),
+            pltpu.VMEM((16, P_SIZE + D), F32),
+            pltpu.VMEM((160, D), BF16),
+            pltpu.VMEM((D, P_SIZE), BF16),
+            pltpu.SemaphoreType.DMA((2,)),
+        ],
         limit=16,
+        left=2,
     )
     parts = lax.all_to_all(parts, PLANE, split_axis=0, concat_axis=0, tiled=True)
-    parts = call(plane_sum_kernel, jax.ShapeDtypeStruct((8, 24, 384), F32), (parts,), limit=16)
+    parts = call(plane_sum_kernel, jax.ShapeDtypeStruct((8, 16, 384), BF16), (parts,), limit=16)
     parts = lax.all_to_all(parts, COLUMN, split_axis=0, concat_axis=0, tiled=True)
     probe_step, refine_step = call(
         step_kernel,
@@ -428,7 +520,8 @@
             jax.ShapeDtypeStruct((9, P_SIZE), F32),
             jax.ShapeDtypeStruct((3, 3, P_SIZE), F32),
         ],
-        (parts, taps, mom_probe, var_probe, mom_refine, var_refine),
+        (parts, w_refine, mom_probe, var_probe, mom_refine, var_refine),
+        [pltpu.VMEM((16, P_SIZE), F32)],
         limit=16,
     )
     return (loss_map, map_grad.reshape(2, 2, COLS, P_SIZE), probe_step, refine_step)

time: 168 us -> 143 us (0.85)
  blocking collectives: 57.6 us -> 24.5 us
  waiting for transfers between devices: 12.7 us -> 32.9 us
  Pallas kernels: 60.3 us -> 46.4 us
  starting transfers between devices: 20.1 us -> 25.5 us
  local copies, waits for them, and re-layouts: 13.1 us -> 8.54 us
    all_to_all x1 -> x0, blocking collectives: 26.5 us -> none  [body(): here = lax.all_to_all(sent, SEQ, split_axis=0, concat_axis=0, tiled=True)]
    all_to_all x0 -> x1, waiting for transfers between devices: none -> 17.7 us  [body(): here = lax.all_to_all(sent, SEQ, split_axis=0, concat_axis=0, tiled=True)]
    pallas_call x10 -> x11, Pallas kernels: 60.3 us -> 46.4 us  [call(): pl.pallas_call(kernel, out_shape=out_shape, in_specs=in_specs, out_specs=...]
    all_to_all x0 -> x1, starting transfers between devices: none -> 9.36 us  [body(): here = lax.all_to_all(sent, SEQ, split_axis=0, concat_axis=0, tiled=True)]
    all_to_all x1, blocking collectives: 14.2 us -> 9.93 us  [body(): lax.all_to_all(parts, COLUMN, split_axis=0, concat_axis=0, tiled=True)]
    unnamed x38 -> x32, local copies, waits for them, and re-layouts: 7.39 us -> 3.95 us
    ppermute x4, starting transfers between devices: 7.1 us -> 4.52 us  [the longest x1 2.57 us: body(): map_far = lax.ppermute(tap_maps, TILE, tile_far)]
    all_to_all x1, blocking collectives: 16.9 us -> 14.6 us  [body(): lax.all_to_all(parts, PLANE, split_axis=0, concat_axis=0, tiled=True)]
  transfers between devices with their start and end apart: 8 -> 9, of which waited for: 3 -> 4; matrix products, arithmetic and copies ran while one was open for 1% -> 1% of each run, Pallas kernels for 23% -> 21%
where the time goes in v2:
time: 143 us; the launch traced here: 142 us
  Pallas kernels  46.4 us (32%)
  waiting for transfers between devices  32.9 us (23%)
  starting transfers between devices  25.5 us (18%)
  blocking collectives  24.5 us (17%)
  local copies, waits for them, and re-layouts  8.54 us (6%)
  other arithmetic  3.53 us (2%)
    pallas_call x11, Pallas kernels, call(): pl.pallas_call(kernel, out_shape=out_shape, in_specs=in_specs, out_specs=...  46.4 us
    all_to_all x1, waiting for transfers between devices, body(): here = lax.all_to_all(sent, SEQ, split_axis=0, concat_axis=0, tiled=True)  17.7 us
    all_to_all x1, blocking collectives, body(): lax.all_to_all(parts, PLANE, split_axis=0, concat_axis=0, tiled=True)  14.6 us
    all_to_all x1, blocking collectives, body(): lax.all_to_all(parts, COLUMN, split_axis=0, concat_axis=0, tiled=True)  9.93 us
    all_to_all x1, waiting for transfers between devices, body(): lax.all_to_all(attended.reshape(SEQ_COUNT, 2, COLS * HD), SEQ, split_axis...  9.8 us
    all_to_all x1, starting transfers between devices, body(): here = lax.all_to_all(sent, SEQ, split_axis=0, concat_axis=0, tiled=True)  9.36 us
    all_to_all x1, starting transfers between devices, body(): lax.all_to_all(attended.reshape(SEQ_COUNT, 2, COLS * HD), SEQ, split_axis...  4.85 us
    unnamed x32, local copies, waits for them, and re-layouts  3.95 us
  transfers between devices with their start and end apart: 9, of which 4 were waited for; matrix products, arithmetic and copies ran while one was open for 1% of the time, Pallas kernels for 21%

profile of v2, /device:TPU:1, one launch (start us, length us, event | category | flops | bytes accessed | tf_op | source)
XLA Modules:
  0.0 142.3 jit_solution(7657649892555901141)
XLA Ops:
  0.6 3.5 %pad_maximum_fusion = bf16[32,3,2,2880]{3,2,1,0:T(2,128)(2,1)} fusion(bf16[32,1,2,2880]{3,2,1,0:T(2,128)(2,1)} %bitcast.18, bf16[32,1,2,2880]{3,2,1,0:T(2,128)(2,1)} %bitcast.19, bf16[32,1,2,2880]{3,2,1,0:T(2,128)(2,1)} %bitcast.20), kind=kLoop, calls=%fused_computation | loop fusion | flops 1105920 | bytes 2211840 | tf_op jit(solution)/shard_map/concatenate | solution.py:444
  4.2 9.4 %all-to-all-start = ((bf16[32,3,2,2880]{3,2,1,0:T(2,128)(2,1)}), bf16[32,3,2,2880]{3,2,1,0:T(2,128)(2,1)S(1)}, u32[]{:S(2)}, u32[]{:S(2)}) async-start(bf16[32,3,2,2880]{3,2,1,0:T(2,128)(2,1)} %pad_maximum_fusion), calls=%async_computation | async-start | bytes 2260992 | tf_op jit(solution)/shard_map/all_to_all | solution.py:445
  13.6 17.7 %all-to-all-done = bf16[32,3,2,2880]{3,2,1,0:T(2,128)(2,1)S(1)} async-done(((bf16[32,3,2,2880]{3,2,1,0:T(2,128)(2,1)}), bf16[32,3,2,2880]{3,2,1,0:T(2,128)(2,1)S(1)}, u32[]{:S(2)}, u32[]{:S(2)}) %all-to-all-start) | async-done | bytes 1105952 | tf_op jit(solution)/shard_map/all_to_all | solution.py:445
  32.7 2.1 %collective-permute-start.1 = (bf16[2,64,2880]{2,1,0:T(8,128)(2,1)S(1)}, bf16[2,64,2880]{2,1,0:T(8,128)(2,1)S(1)}, u32[]{:S(2)}, u32[]{:S(2)}) collective-permute-start(bf16[2,64,2880]{2,1,0:T(8,128)(2,1)S(1)} %constant_dynamic-update-slice_fusion.refs_1_), channel_id=1, source_target_pairs={{0,1},{1,0},{2,3},{3,2},{4,5},{5,4},{6,7},{7,6},{8,9},{9,8},{10,11... | collective-permute-start | bytes 2211848 | tf_op jit(solution)/shard_map/ppermute | solution.py:450
  36.5 3.3 %collective-permute-start = (bf16[2,64,2880]{2,1,0:T(8,128)(2,1)S(1)}, bf16[2,64,2880]{2,1,0:T(8,128)(2,1)S(1)}, u32[]{:S(2)}, u32[]{:S(2)}) collective-permute-start(bf16[2,64,2880]{2,1,0:T(8,128)(2,1)S(1)} %constant_dynamic-update-slice_fusion.refs_1_), channel_id=1, source_target_pairs={{0,2},{2,0},{1,3},{3,1},{4,6},{6,4},{5,7},{7,5},{8,10},{10,8},{9,1... | collective-permute-start | bytes 2211848 | tf_op jit(solution)/shard_map/ppermute | solution.py:449
  40.1 9.0 %shard_map.156 = (bf16[2560,128]{1,0:T(8,128)(2,1)S(1)}, f32[2560,128]{1,0:T(8,128)S(1)}) custom-call(bf16[64,2880]{1,0:T(8,128)(2,1)S(1)} %reshape_squeeze.3.refs_0_, bf16[2,64,2880]{2,1,0:T(8,128)(2,1)S(1)} %constant_dynamic-update-slice_fusion.refs_1_), custom_call_target="tpu_custom_call" | custom-call | flops 6710886400 | bytes 4194304 | tf_op jit(solution)/shard_map/pallas_call | solution.py:61
  49.1 9.4 %shard_map.158.refs_2_ = f32[2560,128]{1,0:T(8,128)S(1)} custom-call(bf16[2560,128]{1,0:T(8,128)(2,1)S(1)} %get-tuple-element.26.refs_0_, bf16[2,64,2880]{2,1,0:T(8,128)(2,1)S(1)} %collective-permute-done.1.refs_1_, f32[2560,128]{1,0:T(8,128)S(1)} %get-tuple-element.31.refs_2_), custom_call_target="tpu_custom_call" | custom-call | flops 6710886400 | bytes 4194304 | tf_op jit(solution)/shard_map/pallas_call | solution.py:61
  58.5 1.4 collective-permute-start.2
  59.9 9.4 %shard_map.159.refs_2_ = f32[2560,128]{1,0:T(8,128)S(1)} custom-call(bf16[2560,128]{1,0:T(8,128)(2,1)S(1)} %get-tuple-element.26.refs_0_, bf16[2,64,2880]{2,1,0:T(8,128)(2,1)S(1)} %collective-permute-done.refs_1_, f32[2560,128]{1,0:T(8,128)S(1)} %shard_map.158.refs_2_), custom_call_target="tpu_custom_call" | custom-call | flops 6710886400 | bytes 4194304 | tf_op jit(solution)/shard_map/pallas_call | solution.py:61
  69.4 9.8 %shard_map.160 = bf16[64,2880]{1,0:T(8,128)(2,1)S(1)} custom-call(bf16[2560,128]{1,0:T(8,128)(2,1)S(1)} %get-tuple-element.26.refs_0_, bf16[2,64,2880]{2,1,0:T(8,128)(2,1)S(1)} %collective-permute-done.2.refs_1_, f32[2560,128]{1,0:T(8,128)S(1)} %shard_map.159.refs_2_), custom_call_target="tpu_custom_call" | custom-call | flops 6710886400 | bytes 4194304 | tf_op jit(solution)/shard_map/pallas_call | solution.py:61
  80.1 4.8 %all-to-all-start.1 = ((bf16[32,2,2880]{2,1,0:T(2,128)(2,1)}), bf16[32,2,2880]{2,1,0:T(2,128)(2,1)}, u32[]{:S(2)}, u32[]{:S(2)}) async-start(bf16[32,2,2880]{2,1,0:T(2,128)(2,1)} %reshape.43), calls=%async_computation.1 | async-start | bytes 753664 | tf_op jit(solution)/shard_map/all_to_all | solution.py:458
  85.7 9.8 %all-to-all-done.1 = bf16[32,2,2880]{2,1,0:T(2,128)(2,1)} async-done(((bf16[32,2,2880]{2,1,0:T(2,128)(2,1)}), bf16[32,2,2880]{2,1,0:T(2,128)(2,1)}, u32[]{:S(2)}, u32[]{:S(2)}) %all-to-all-start.1) | async-done | bytes 368672 | tf_op jit(solution)/shard_map/all_to_all | solution.py:458
  95.5 1.3 reshape.44.merged
  97.5 2.8 %shard_map.161 = (bf16[160,1152]{1,0:T(8,128)(2,1)S(1)}, f32[48,384]{1,0:T(8,128)}) custom-call(bf16[64,2880]{1,0:T(8,128)(2,1)S(1)} %reshape.44.merged, bf16[160,1152]{1,0:T(8,128)(2,1)S(1)} %bitcast.15, f32[1,1152]{1,0:T(1,128)S(1)} %reshape.46.gate, bf16[1152,1152]{1,0:T(8,128)(2,1)S(1)} %copy-done, bf16[48,1152]{1,0:T(8,128)(2,1)S(1)} %get-tuple-element.34.tap_weights, ...), custom_call_target="tpu_custom_call" | custom-call | tf_op jit(solution)/shard_map/pallas_call | solution.py:61
  101.0 1.1 collective-permute-start.3
  102.1 2.6 %collective-permute-start.4 = (f32[48,384]{1,0:T(8,128)}, f32[48,384]{1,0:T(8,128)S(1)}, u32[]{:S(2)}, u32[]{:S(2)}) collective-permute-start(f32[48,384]{1,0:T(8,128)} %get-tuple-element.36.own), channel_id=1, source_target_pairs={{1,2},{2,1},{5,6},{6,5},{9,10},{10,9},{13,14},{14,13},{17,18},{18,... | collective-permute-start | bytes 221192 | tf_op jit(solution)/shard_map/ppermute | solution.py:479
  104.8 1.3 shard_map.162
  106.1 3.3 %collective-permute-done.4.far = f32[48,384]{1,0:T(8,128)S(1)} collective-permute-done((f32[48,384]{1,0:T(8,128)}, f32[48,384]{1,0:T(8,128)S(1)}, u32[]{:S(2)}, u32[]{:S(2)}) %collective-permute-start.4) | collective-permute-done | bytes 73760 | tf_op jit(solution)/shard_map/ppermute | solution.py:479
  111.1 2.1 %collective-permute-done.5.near = f32[48,256]{1,0:T(8,128)S(1)} collective-permute-done((f32[48,256]{1,0:T(8,128)S(1)}, f32[48,256]{1,0:T(8,128)S(1)}, u32[]{:S(2)}, u32[]{:S(2)}) %collective-permute-start.5) | collective-permute-done | bytes 49184 | tf_op jit(solution)/shard_map/ppermute | solution.py:495
  113.2 1.0 copy-done.6
  114.2 2.5 %shard_map.164 = (f32[2,8,160]{2,1,0:T(8,128)}, bf16[160,256]{1,0:T(8,128)(2,1)}, bf16[16,16,384]{2,1,0:T(8,128)(2,1)S(1)}) custom-call(s32[6]{0:T(128)S(1)} %stack.30.place, f32[48,256]{1,0:T(8,128)S(1)} %shard_map.163.own, f32[48,256]{1,0:T(8,128)S(1)} %collective-permute-done.5.near, f32[48,256]{1,0:T(8,128)S(1)} %collective-permute-done.6.far, ...), custom_call_target="tpu_custom_call" | custom-call | tf_op jit(solution)/shard_map/pallas_call | solution.py:61
  116.8 14.6 %all_to_all.20.parts = bf16[16,16,384]{2,1,0:T(8,128)(2,1)S(1)} all-to-all(bf16[16,16,384]{2,1,0:T(8,128)(2,1)S(1)} %get-tuple-element.45), channel_id=1, replica_groups=mesh['y'=4,'x'=4,'z_lo'=2,'z_hi'=2,'core'=2] {'y','x'}, dimensions={0} | all-to-all | bytes 393216 | tf_op jit(solution)/shard_map/all_to_all | solution.py:514
  131.4 9.9 %all_to_all.21.parts = bf16[8,16,384]{2,1,0:T(8,128)(2,1)S(1)} all-to-all(bf16[8,16,384]{2,1,0:T(8,128)(2,1)S(1)} %shard_map.165), channel_id=1, replica_groups=mesh['y'=4,'x'=4,'z_lo'=2,'z_hi'=2,'core'=2] {'z_lo','z_hi','core'}, dimensions={0} | all-to-all | bytes 196608 | tf_op jit(solution)/shard_map/all_to_all | solution.py:516
  141.4 0.9 shard_map.166
  (50 shorter events, 8.3 us)
Async XLA Ops:
  4.2 9.4 %copy-start.7 = (f32[3,3,256]{2,1,0:T(4,128)S(1)}, f32[3,3,256]{2,1,0:T(4,128)}, u32[]{:S(2)}) copy-start(f32[3,3,256]{2,1,0:T(4,128)} %w_refine.1) | copy-start | bytes 27652
  4.2 27.0 %all-to-all-start = ((bf16[32,3,2,2880]{3,2,1,0:T(2,128)(2,1)}), bf16[32,3,2,2880]{3,2,1,0:T(2,128)(2,1)S(1)}, u32[]{:S(2)}, u32[]{:S(2)}) async-start(bf16[32,3,2,2880]{3,2,1,0:T(2,128)(2,1)} %pad_maximum_fusion), calls=%async_computation | async-start | bytes 2260992 | tf_op jit(solution)/shard_map/all_to_all | solution.py:445
  32.3 2.5 %copy-start.1 = (f32[1152,256]{1,0:T(8,128)S(1)}, f32[1152,256]{1,0:T(8,128)}, u32[]{:S(2)}) copy-start(f32[1152,256]{1,0:T(8,128)} %w_probe.1) | copy-start | bytes 3538948
  32.3 2.5 %copy-start.8 = (s32[2,8,160]{2,1,0:T(8,128)S(1)}, s32[2,8,160]{2,1,0:T(8,128)}, u32[]{:S(2)}) copy-start(s32[2,8,160]{2,1,0:T(8,128)} %param.21) | copy-start | bytes 30724
  32.7 16.4 %collective-permute-start.1 = (bf16[2,64,2880]{2,1,0:T(8,128)(2,1)S(1)}, bf16[2,64,2880]{2,1,0:T(8,128)(2,1)S(1)}, u32[]{:S(2)}, u32[]{:S(2)}) collective-permute-start(bf16[2,64,2880]{2,1,0:T(8,128)(2,1)S(1)} %constant_dynamic-update-slice_fusion.refs_1_), channel_id=1, source_target_pairs={{0,1},{1,0},{2,3},{3,2},{4,5},{5,4},{6,7},{7,6},{8,9},{9,8},{10,11... | collective-permute-start | bytes 2211848 | tf_op jit(solution)/shard_map/ppermute | solution.py:450
  35.1 0.8 copy-start.2
  35.9 0.6 copy-start.11
  36.5 22.0 %collective-permute-start = (bf16[2,64,2880]{2,1,0:T(8,128)(2,1)S(1)}, bf16[2,64,2880]{2,1,0:T(8,128)(2,1)S(1)}, u32[]{:S(2)}, u32[]{:S(2)}) collective-permute-start(bf16[2,64,2880]{2,1,0:T(8,128)(2,1)S(1)} %constant_dynamic-update-slice_fusion.refs_1_), channel_id=1, source_target_pairs={{0,2},{2,0},{1,3},{3,1},{4,6},{6,4},{5,7},{7,5},{8,10},{10,8},{9,1... | collective-permute-start | bytes 2211848 | tf_op jit(solution)/shard_map/ppermute | solution.py:449
  58.5 10.8 %collective-permute-start.2 = (bf16[2,64,2880]{2,1,0:T(8,128)(2,1)S(1)}, bf16[2,64,2880]{2,1,0:T(8,128)(2,1)S(1)}, u32[]{:S(2)}, u32[]{:S(2)}) collective-permute-start(bf16[2,64,2880]{2,1,0:T(8,128)(2,1)S(1)} %collective-permute-done.refs_1_), channel_id=1, source_target_pairs={{0,1},{1,0},{2,3},{3,2},{4,5},{5,4},{6,7},{7,6},{8,9},{9,8},{10,11... | collective-permute-start | bytes 2211848 | tf_op jit(solution)/shard_map/ppermute | solution.py:455
  69.3 27.4 %copy-start = (bf16[1152,1152]{1,0:T(8,128)(2,1)S(1)}, bf16[1152,1152]{1,0:T(8,128)(2,1)}, u32[]{:S(2)}) copy-start(bf16[1152,1152]{1,0:T(8,128)(2,1)} %w_out.1) | copy-start | bytes 7962628
  79.2 17.5 %copy-start.4 = (bf16[2,2,40,1152]{3,2,1,0:T(8,128)(2,1)S(1)}, bf16[2,2,40,1152]{3,2,1,0:T(8,128)(2,1)}, u32[]{:S(2)}) copy-start(bf16[2,2,40,1152]{3,2,1,0:T(8,128)(2,1)} %param.16) | copy-start | bytes 1105924
  80.1 15.4 %all-to-all-start.1 = ((bf16[32,2,2880]{2,1,0:T(2,128)(2,1)}), bf16[32,2,2880]{2,1,0:T(2,128)(2,1)}, u32[]{:S(2)}, u32[]{:S(2)}) async-start(bf16[32,2,2880]{2,1,0:T(2,128)(2,1)} %reshape.43), calls=%async_computation.1 | async-start | bytes 753664 | tf_op jit(solution)/shard_map/all_to_all | solution.py:458
  96.7 0.7 copy-start.12
  100.3 0.7 copy-start.5
  101.0 12.2 %copy-start.3 = (bf16[1152,256]{1,0:T(8,128)(2,1)S(1)}, bf16[1152,256]{1,0:T(8,128)(2,1)}, u32[]{:S(2)}) copy-start(bf16[1152,256]{1,0:T(8,128)(2,1)} %copy-done.2) | copy-start | bytes 1769476
  101.0 5.1 %collective-permute-start.3 = (f32[48,384]{1,0:T(8,128)}, f32[48,384]{1,0:T(8,128)S(1)}, u32[]{:S(2)}, u32[]{:S(2)}) collective-permute-start(f32[48,384]{1,0:T(8,128)} %get-tuple-element.36.own), channel_id=1, source_target_pairs={{0,1},{1,0},{2,3},{3,2},{4,5},{5,4},{6,7},{7,6},{8,9},{9,8},{10,11... | collective-permute-start | bytes 221192 | tf_op jit(solution)/shard_map/ppermute | solution.py:480
  102.1 7.4 %collective-permute-start.4 = (f32[48,384]{1,0:T(8,128)}, f32[48,384]{1,0:T(8,128)S(1)}, u32[]{:S(2)}, u32[]{:S(2)}) collective-permute-start(f32[48,384]{1,0:T(8,128)} %get-tuple-element.36.own), channel_id=1, source_target_pairs={{1,2},{2,1},{5,6},{6,5},{9,10},{10,9},{13,14},{14,13},{17,18},{18,... | collective-permute-start | bytes 221192 | tf_op jit(solution)/shard_map/ppermute | solution.py:479
  109.5 31.9 %copy-start.9 = (f32[9,256]{1,0:T(8,128)S(1)}, f32[9,256]{1,0:T(8,128)}, u32[]{:S(2)}) copy-start(f32[9,256]{1,0:T(8,128)} %mom_probe.1) | copy-start | bytes 27652
  109.5 31.9 %copy-start.10 = (f32[9,256]{1,0:T(8,128)S(1)}, f32[9,256]{1,0:T(8,128)}, u32[]{:S(2)}) copy-start(f32[9,256]{1,0:T(8,128)} %var_probe.1) | copy-start | bytes 27652
  109.5 31.9 %copy-start.13 = (f32[3,3,256]{2,1,0:T(4,128)S(1)}, f32[3,3,256]{2,1,0:T(4,128)}, u32[]{:S(2)}) copy-start(f32[3,3,256]{2,1,0:T(4,128)} %mom_refine.1) | copy-start | bytes 27652
  109.5 31.9 %copy-start.14 = (f32[3,3,256]{2,1,0:T(4,128)S(1)}, f32[3,3,256]{2,1,0:T(4,128)}, u32[]{:S(2)}) copy-start(f32[3,3,256]{2,1,0:T(4,128)} %var_refine.1) | copy-start | bytes 27652
  110.2 3.0 %collective-permute-start.5 = (f32[48,256]{1,0:T(8,128)S(1)}, f32[48,256]{1,0:T(8,128)S(1)}, u32[]{:S(2)}, u32[]{:S(2)}) collective-permute-start(f32[48,256]{1,0:T(8,128)S(1)} %shard_map.163.own), channel_id=1, source_target_pairs={{0,4},{4,0},{8,12},{12,8},{16,20},{20,16},{24,28},{28,24},{32,36},... | collective-permute-start | bytes 147464 | tf_op jit(solution)/shard_map/ppermute | solution.py:495
  110.4 2.8 %collective-permute-start.6 = (f32[48,256]{1,0:T(8,128)S(1)}, f32[48,256]{1,0:T(8,128)S(1)}, u32[]{:S(2)}, u32[]{:S(2)}) collective-permute-start(f32[48,256]{1,0:T(8,128)S(1)} %shard_map.163.own), channel_id=1, source_target_pairs={{4,8},{8,4},{12,16},{16,12},{20,24},{24,20},{28,32},{32,28},{36,40... | collective-permute-start | bytes 147464 | tf_op jit(solution)/shard_map/ppermute | solution.py:494
  113.2 1.0 copy-start.6
